TPU v7x, 512 devices: a whole 4x8x8 slice. The times are simulated.
512 devices in a mesh: tok: 128 (over z, y, core), head: 4 (over x).
Axes of the slice: x: 4, y: 8, z: 8, core: 2. Of those that a mesh axis runs over, the one named last changes fastest.
Arguments:
- queries: bfloat16 [32768, 3072], P(('tok', 'head')), may hold values from -9 to 9
- key_rows: bfloat16 [32768, 3072], P(('tok', 'head')), may hold values from -13.5 to 13.5
- values: bfloat16 [32768, 3072], P(('tok', 'head')), may hold values from -6 to 6
- cluster: int32 [32768], P('tok'), may hold values from 0 to 511, as said below
- owners: int32 [512], replicated, may hold values from 0 to 511, as said below
- pair_list: int32 [512, 8], P('tok'), may hold values from 0 to 511, as said below
Outputs:
- attended: bfloat16 [32768, 3072], P(('tok', 'head'))
Inputs may be any that keep to these rules, and one draw needn't show every extreme that they name: Of the tokens of one tok index (aligned blocks of 256), at most 4 are in clusters whose slot lies on one owner (owners[c] // 4); at most 128 tokens share a cluster; both bounds are reached in every draw. A permutation: cluster c sits in slot owners[c], which is local cluster owners[c] % 4 of tok index owners[c] // 4. `pair_list`: row s starts with s; its other entries are distinct, differ from s, and are slots of tok indices s // 4 - 1 to s // 4 + 1.
All inputs are finite; a program needn't handle non-finite values.
Results may differ from a plain program's by a relative error of at most 0.0026.
Values may be sent and summed in bfloat16 or wider, within the bound.
A program may use at most 64 MiB of HBM per device.

v0:
```python
import functools
import math

import jax
import jax.numpy as jnp
from jax import lax
from jax.experimental import pallas as pl
from jax.experimental.pallas import tpu as pltpu
from jax.sharding import PartitionSpec as P

HEAD_DIM = 128
CAP = 128
CORES = 2
SWAP = 1
LAG = 2
MASKED = -(2.0**100)
SCALE_LOG2 = math.log2(math.e) / math.sqrt(HEAD_DIM)
MESH = pl.DeviceIdType.MESH
F32 = jnp.float32
BF16 = jnp.bfloat16

X_OWN, X_SEND, X_RECV, A_SEND, A_RECV, B_SEND, B_RECV, H_SEND, H_RECV = range(9)
RB_SEND, RB_RECV, RA_SEND, RA_RECV, RX_SEND, RX_OWN = range(9, 15)
STAGES = 15


def matmul(left, right):
    return jnp.dot(left, right, preferred_element_type=F32)


def matmul_t(left, right):
    return lax.dot_general(left, right, (((1,), (1,)), ((), ())), preferred_element_type=F32)


def iota(shape, dim):
    return lax.broadcasted_iota(jnp.int32, shape, dim)


def one_hot(condition):
    return jnp.where(condition, 1.0, 0.0).astype(BF16)


def wait_bytes(ref, sem):
    pltpu.make_async_copy(ref, ref, sem).wait()


def kernel(
    dims, q_ref, k_ref, v_ref, cluster, owners, pair_list, out_ref,
    x_recv, a_send, a_recv, b_send, b_recv, halo, o_send, o_recv, t_send, t_recv, x_back,
    pick, pick_t, perm, perm_t,
    l_a_send, l_a_recv, l_b_send, l_b_recv, l_halo, mask_in, q_mask, k_mask, mask_tile,
    sem, label_sem, out_sem, mask_sem,
):
    nx, n_axis, per_pair, heads = dims
    tokens = nx * q_ref.shape[0]
    rows = q_ref.shape[0]
    slots = n_axis * n_axis * CORES * per_pair
    width = heads * HEAD_DIM
    line = n_axis * CORES
    a_rows = line * per_pair
    b_rows = n_axis * per_pair
    n_tok = n_axis * line
    pars = 1 + SWAP
    my_x = lax.axis_index("head")
    tok = lax.axis_index("tok")
    z, y, core = tok // line, (tok // CORES) % n_axis, tok % CORES

    def place(par):
        return z + par * (y - z), y + par * (z - y), core + par * (1 - 2 * core)

    def device(a, b, c, par):
        return (
            (a + par * (b - a)) * line + (b + par * (a - b)) * CORES + c + par * (1 - 2 * c),
            my_x,
        )

    def device_of(owner, par):
        return device(owner // line, (owner // CORES) % n_axis, owner % CORES, par)

    def neighbour(par, step):
        a, b, c = place(par)
        owner = (a * n_axis + b) * CORES + c
        return device_of(lax.rem(owner + step + n_tok, n_tok), par)

    def copy_to(src, dst, send, recv, target):
        return pltpu.make_async_remote_copy(
            src_ref=src, dst_ref=dst, send_sem=send, recv_sem=recv,
            device_id=target, device_id_type=MESH,
        )

    def lanes(start, size):
        return pl.ds(pl.multiple_of(start, HEAD_DIM), size)

    def block(index, size):
        return pl.ds(pl.multiple_of(index * size, size), size)

    barrier = pltpu.get_barrier_semaphore()

    def greet(target):
        pl.semaphore_signal(barrier, inc=1, device_id=target, device_id_type=MESH)

    @pl.loop(1, nx)
    def _(d):
        greet((tok, lax.rem(my_x + d, nx)))

    @pl.loop(1, line)
    def _(d):
        greet((z * line + lax.rem(y * CORES + core + d, line), my_x))

    @pl.loop(1, n_axis)
    def _(d):
        other = lax.rem(z + d, n_axis)
        for c in range(CORES):
            greet(((other * n_axis + y) * CORES + c, my_x))

    for par in range(pars):
        greet(neighbour(par, 1))
        greet(neighbour(par, -1))
    greeted = (nx - 1) + (line - 1) + (n_axis - 1) * CORES + 2 * pars
    if SWAP:
        partner = device(z, y, core, 1)
        greet(partner)
        greeted += 1

    def own_copy(ref, kind, h):
        return pltpu.make_async_copy(
            ref.at[:, lanes(my_x * width + h * HEAD_DIM, HEAD_DIM)],
            x_recv.at[h, block(my_x, rows), pl.ds(kind * HEAD_DIM, HEAD_DIM)],
            sem.at[X_OWN, h],
        )

    @pl.loop(0, heads)
    def _(h):
        for kind, ref in enumerate((q_ref, k_ref, v_ref)):
            own_copy(ref, kind, h).start()

    tile = mask_tile.shape[0]
    cl_dev, pairs = pair_list.shape
    pair_local = pair_list[...] - (tok - 1) * cl_dev
    lane = iota((cl_dev, HEAD_DIM), 1)
    allowed = lane > 3 * cl_dev
    for j in range(pairs):
        allowed = allowed | (pair_local[:, j : j + 1] == lane)
    pair_mask = jnp.where(allowed, 0.0, MASKED)
    mask_tile[...] = jnp.concatenate(
        [pair_mask, jnp.zeros((tile - cl_dev, HEAD_DIM), F32)], axis=0
    ).astype(BF16)
    pl.semaphore_wait(barrier, greeted)

    @pl.loop(0, heads)
    def _(h):
        for d in range(1, nx):
            other = lax.rem(my_x + d, nx)
            for kind, ref in enumerate((q_ref, k_ref, v_ref)):
                copy_to(
                    ref.at[:, lanes(other * width + h * HEAD_DIM, HEAD_DIM)],
                    x_recv.at[h, block(my_x, rows), pl.ds(kind * HEAD_DIM, HEAD_DIM)],
                    sem.at[X_SEND, h],
                    sem.at[X_RECV, h],
                    (tok, other),
                ).start()

    if SWAP:
        mask_copy = copy_to(mask_tile, mask_in, mask_sem.at[0], mask_sem.at[1], partner)
        mask_copy.start()

    clusters = owners.shape[1]
    cluster_hot = one_hot(iota((clusters, tokens), 0) == cluster[...])
    table = jnp.where(
        iota((tile, clusters), 0) == 0, owners[...] // cl_dev, owners[...] % cl_dev
    )
    found = matmul(table.astype(F32).astype(BF16), cluster_hot).astype(jnp.int32)
    target, local_id = found[0:1], found[1:2]
    target_hot = one_hot(iota((n_tok, tokens), 0) == target)
    earlier = one_hot(iota((tokens, tokens), 0) < iota((tokens, tokens), 1))
    rank = jnp.sum(matmul(target_hot, earlier) * target_hot.astype(F32), axis=0, keepdims=True)
    pos = target * per_pair + rank.astype(jnp.int32)
    pick[...] = one_hot(iota((slots, tokens), 0) == pos)
    same = one_hot(iota((tokens, tokens), 0) == iota((tokens, tokens), 1))
    pick_t[...] = matmul_t(same, pick[...]).astype(BF16)
    lane = iota((HEAD_DIM, tokens), 0)
    labels = matmul_t(pick[...], one_hot((lane == local_id) | (lane == cl_dev)))
    lane = iota((slots, HEAD_DIM), 1)
    l_a_send[...] = jnp.where(lane == cl_dev, 1.0 - labels, labels).astype(BF16)

    def first_hop(src, dst, send, recv, par):
        a, b, c = place(par)

        @pl.loop(1, n_axis)
        def _(d):
            other = lax.rem(a + d, n_axis)
            copy_to(
                src.at[block(other, a_rows)], dst.at[block(a, a_rows)], send, recv,
                device(other, b, c, par),
            ).start()

    def second_hop(src, dst, send, recv, par):
        a, b, c = place(par)
        here = b * CORES + c

        @pl.loop(1, line)
        def _(d):
            other = lax.rem(here + d, line)
            copy_to(
                src.at[block(other, b_rows)], dst.at[block(here, b_rows)], send, recv,
                device(a, other // CORES, other % CORES, par),
            ).start()

    others_a = pl.ds(0, slots - a_rows)
    others_b = pl.ds(0, slots - b_rows)

    def keep_a(src, dst, par):
        a, _, _ = place(par)
        dst[block(a, a_rows)] = src[block(a, a_rows)]

    def keep_b(src, dst, par):
        _, b, c = place(par)
        dst[block(b * CORES + c, b_rows)] = src[block(b * CORES + c, b_rows)]

    for par in range(pars):
        first_hop(
            l_a_send, l_a_recv.at[par], label_sem.at[0, par], label_sem.at[1, par], par
        )
        keep_a(l_a_send, l_a_recv.at[par], par)

    out_row, in_row = iota((slots, slots), 0), iota((slots, slots), 1)

    def source_of(row):
        r, a, bc = row % per_pair, (row // per_pair) % n_axis, row // b_rows
        return a * a_rows + bc * per_pair + r

    perm[...] = one_hot(source_of(out_row) == in_row)
    perm_t[...] = one_hot(source_of(in_row) == out_row)

    def pack(h):
        par = SWAP * (h % 2)
        for kind, ref in enumerate((q_ref, k_ref, v_ref)):
            own_copy(ref, kind, h).wait()
        wait_bytes(x_recv.at[h, pl.ds(0, tokens - rows)], sem.at[X_RECV, h])
        a_send[h] = matmul(pick[...], x_recv[h]).astype(BF16)
        first_hop(a_send.at[h], a_recv.at[h], sem.at[A_SEND, h], sem.at[A_RECV, h], par)
        keep_a(a_send.at[h], a_recv.at[h], par)

    def turn(h):
        par = SWAP * (h % 2)
        wait_bytes(a_recv.at[h, others_a], sem.at[A_RECV, h])
        b_send[h] = matmul(perm[...], a_recv[h]).astype(BF16)
        second_hop(b_send.at[h], b_recv.at[h], sem.at[B_SEND, h], sem.at[B_RECV, h], par)
        keep_b(b_send.at[h], b_recv.at[h], par)

    def share(h):
        par = SWAP * (h % 2)
        wait_bytes(b_recv.at[h, others_b], sem.at[B_RECV, h])
        for side, step in ((0, 1), (1, -1)):
            copy_to(
                b_recv.at[h, :, pl.ds(HEAD_DIM, 2 * HEAD_DIM)], halo.at[h, side],
                sem.at[H_SEND, h], sem.at[H_RECV, h], neighbour(par, step),
            ).start()

    query_rows = min(256, slots)

    def attend(h):
        par = SWAP * (h % 2)
        wait_bytes(halo.at[h], sem.at[H_RECV, h])

        @pl.loop(0, slots // query_rows)
        def _(step):
            here = block(step, query_rows)
            query = jnp.concatenate(
                [b_recv[h, here, 0:HEAD_DIM], q_mask[par, here]], axis=1
            )
            scores = []
            for part in range(3):
                if part == 1:
                    key = b_recv[h, :, HEAD_DIM : 2 * HEAD_DIM]
                else:
                    key = halo[h, part // 2, :, 0:HEAD_DIM]
                key = jnp.concatenate([key, k_mask[par, part]], axis=1)
                scores.append(matmul_t(query, key))
            row_max = functools.reduce(
                jnp.maximum, [jnp.max(s, axis=1, keepdims=True) for s in scores]
            )
            total, mixed = 0.0, 0.0
            for part in range(3):
                weights = jnp.exp2((scores[part] - row_max) * SCALE_LOG2)
                total = total + jnp.sum(weights, axis=1, keepdims=True)
                if part == 1:
                    value = b_recv[h, :, 2 * HEAD_DIM : 3 * HEAD_DIM]
                else:
                    value = halo[h, part // 2, :, HEAD_DIM : 2 * HEAD_DIM]
                mixed = mixed + matmul(weights.astype(BF16), value)
            o_send[h, here] = (mixed / total).astype(BF16)

        second_hop(o_send.at[h], o_recv.at[h], sem.at[RB_SEND, h], sem.at[RB_RECV, h], par)
        keep_b(o_send.at[h], o_recv.at[h], par)

    def turn_back(h):
        par = SWAP * (h % 2)
        wait_bytes(o_recv.at[h, others_b], sem.at[RB_RECV, h])
        t_send[h] = matmul(perm_t[...], o_recv[h]).astype(BF16)
        first_hop(t_send.at[h], t_recv.at[h], sem.at[RA_SEND, h], sem.at[RA_RECV, h], par)
        keep_a(t_send.at[h], t_recv.at[h], par)

    def finish(h):
        wait_bytes(t_recv.at[h, others_a], sem.at[RA_RECV, h])
        x_back[h] = matmul(pick_t[...], t_recv[h]).astype(BF16)
        column = lanes(my_x * width + h * HEAD_DIM, HEAD_DIM)
        pltpu.make_async_copy(
            x_back.at[h, block(my_x, rows)], out_ref.at[:, column], sem.at[RX_OWN, h]
        ).start()
        for d in range(1, nx):
            other = lax.rem(my_x + d, nx)
            copy_to(
                x_back.at[h, block(other, rows)], out_ref.at[:, column],
                sem.at[RX_SEND, h], out_sem, (tok, other),
            ).start()

    def turn_labels():
        for par in range(pars):
            wait_bytes(l_a_recv.at[par, others_a], label_sem.at[1, par])
            l_b_send[par] = matmul(perm[...], l_a_recv[par]).astype(BF16)
            second_hop(
                l_b_send.at[par], l_b_recv.at[par],
                label_sem.at[2, par], label_sem.at[3, par], par,
            )
            keep_b(l_b_send.at[par], l_b_recv.at[par], par)

    def share_labels():
        for par in range(pars):
            wait_bytes(l_b_recv.at[par, others_b], label_sem.at[3, par])
            for side, step in ((0, 1), (1, -1)):
                copy_to(
                    l_b_recv.at[par], l_halo.at[par, side],
                    label_sem.at[4, par], label_sem.at[5, par], neighbour(par, step),
                ).start()

    def make_masks():
        row, column = iota((HEAD_DIM, HEAD_DIM), 0), iota((HEAD_DIM, HEAD_DIM), 1)
        if SWAP:
            mask_copy.wait()
        for par in range(pars):
            wait_bytes(l_halo.at[par], label_sem.at[5, par])
            mask = (mask_in if par else mask_tile)[...]
            mask = jnp.concatenate([mask, jnp.zeros((HEAD_DIM - tile, HEAD_DIM), BF16)], axis=0)
            q_mask[par] = matmul(l_b_recv[par], mask).astype(BF16)
            for part in range(3):
                shift = one_hot(
                    ((row < cl_dev) & (column == row + cl_dev * part))
                    | ((row == cl_dev) & (column == 3 * cl_dev))
                )
                label = l_b_recv[par] if part == 1 else l_halo[par, part // 2]
                k_mask[par, part] = matmul(label, shift).astype(BF16)

    stages = (pack, turn, share, attend, turn_back, finish)

    @pl.loop(0, heads + LAG * (len(stages) - 1))
    def _(step):
        for number, stage in enumerate(stages):
            lag = LAG * number

            @pl.when((step >= lag) & (step < heads + lag))
            def _():
                stage(step - lag)

        for number, stage in enumerate((turn_labels, share_labels, make_masks)):

            @pl.when(step == number)
            def _():
                stage()

    everyone = out_ref.at[:, pl.ds(0, (nx - 1) * width)]
    wait_bytes(everyone, out_sem)

    @pl.loop(0, heads)
    def _(h):
        wait_bytes(x_recv.at[h, pl.ds(0, tokens - rows)], sem.at[X_SEND, h])
        wait_bytes(a_send.at[h, others_a], sem.at[A_SEND, h])
        wait_bytes(b_send.at[h, others_b], sem.at[B_SEND, h])
        wait_bytes(halo.at[h], sem.at[H_SEND, h])
        wait_bytes(o_send.at[h, others_b], sem.at[RB_SEND, h])
        wait_bytes(t_send.at[h, others_a], sem.at[RA_SEND, h])
        wait_bytes(x_back.at[h, pl.ds(0, tokens - rows)], sem.at[RX_SEND, h])
        wait_bytes(x_back.at[h, pl.ds(0, rows)], sem.at[RX_OWN, h])

    for par in range(pars):
        wait_bytes(l_a_send.at[others_a], label_sem.at[0, par])
        wait_bytes(l_b_send.at[par, others_b], label_sem.at[2, par])
        wait_bytes(l_halo.at[par], label_sem.at[4, par])


def per_device(queries, key_rows, values, cluster, owners, pair_list):
    nx, n_tok = lax.axis_size("head"), lax.axis_size("tok")
    n_axis = math.isqrt(n_tok // CORES)
    cl_dev = pair_list.shape[0]
    per_pair = CAP * cl_dev // n_tok
    rows, features = queries.shape
    heads = features // nx // HEAD_DIM
    tokens = rows * nx
    slots = n_tok * per_pair
    tile = 16

    pars = 1 + SWAP
    wide, thin = 3 * HEAD_DIM, HEAD_DIM

    def vmem(*shape):
        return pltpu.VMEM(shape, BF16)

    return pl.pallas_call(
        functools.partial(kernel, (nx, n_axis, per_pair, heads)),
        out_shape=jax.ShapeDtypeStruct((rows, features), BF16),
        in_specs=[pl.BlockSpec(memory_space=pltpu.HBM)] * 3
        + [pl.BlockSpec(memory_space=pltpu.VMEM)] * 3,
        out_specs=pl.BlockSpec(memory_space=pltpu.HBM),
        scratch_shapes=[
            vmem(heads, tokens, wide),
            vmem(heads, slots, wide),
            vmem(heads, slots, wide),
            vmem(heads, slots, wide),
            vmem(heads, slots, wide),
            vmem(heads, 2, slots, 2 * HEAD_DIM),
            vmem(heads, slots, thin),
            vmem(heads, slots, thin),
            vmem(heads, slots, thin),
            vmem(heads, slots, thin),
            vmem(heads, tokens, thin),
            vmem(slots, tokens),
            vmem(tokens, slots),
            vmem(slots, slots),
            vmem(slots, slots),
            vmem(slots, thin),
            vmem(pars, slots, thin),
            vmem(pars, slots, thin),
            vmem(pars, slots, thin),
            vmem(pars, 2, slots, thin),
            vmem(tile, thin),
            vmem(pars, slots, thin),
            vmem(pars, 3, slots, thin),
            vmem(tile, thin),
            pltpu.SemaphoreType.DMA((STAGES, heads)),
            pltpu.SemaphoreType.DMA((6, pars)),
            pltpu.SemaphoreType.DMA,
            pltpu.SemaphoreType.DMA((2,)),
        ],
        compiler_params=pltpu.CompilerParams(
            collective_id=0, has_side_effects=True, vmem_limit_bytes=60 * 2**20
        ),
    )(queries, key_rows, values, cluster[None, :], owners[None, :], pair_list)


def solution(mesh):
    return jax.shard_map(
        per_device,
        mesh=mesh,
        in_specs=(
            P(("tok", "head"), None),
            P(("tok", "head"), None),
            P(("tok", "head"), None),
            P("tok"),
            P(),
            P("tok", None),
        ),
        out_specs=P(("tok", "head"), None),
        check_vma=False,
    )
```

profile of v0, /device:TPU:1, one launch (start us, length us, event | category | flops | bytes accessed | tf_op | source)
XLA Modules:
  0.0 127.1 jit_solution(13437723192379584911)
XLA Ops:
  0.0 125.4 %shard_map.64 = bf16[64,3072]{1,0:T(8,128)(2,1)} custom-call(bf16[64,3072]{1,0:T(8,128)(2,1)} %q_ref.1, bf16[64,3072]{1,0:T(8,128)(2,1)} %k_ref.1, bf16[64,3072]{1,0:T(8,128)(2,1)} %v_ref.1, s32[1,256]{1,0:T(1,128)} %bitcast.3, s32[1,512]{1,0:T(1,128)} %bitcast.2, s32[4,8]{1,0:T(4,128)} %pair_list.1), custom_call_target="tpu_custom_call" | custom-call | tf_op jit(solution)/shard_map/pallas_call | solution.py:408
  125.4 1.8 %copy.8 = bf16[64,3072]{1,0:T(8,128)(2,1)} copy(bf16[64,3072]{1,0:T(8,128)(2,1)} %shard_map.64) | data formatting | bytes 786432
where the time goes:
time: 128 us; the launch traced here: 127 us
  Pallas kernels  125 us (98%)
  local copies, waits for them, and re-layouts  1.77 us (1%)
    pallas_call x1, Pallas kernels, per_device(): pl.pallas_call(functools.partial(kernel, (nx, n_axis, per_pair, heads)),...  125 us

commit v1 on v0

--- a/solution.py
+++ b/solution.py
@@ -12,7 +12,6 @@
 CAP = 128
 CORES = 2
 SWAP = 1
-LAG = 2
 MASKED = -(2.0**100)
 SCALE_LOG2 = math.log2(math.e) / math.sqrt(HEAD_DIM)
 MESH = pl.DeviceIdType.MESH
@@ -21,7 +20,8 @@
 
 X_OWN, X_SEND, X_RECV, A_SEND, A_RECV, B_SEND, B_RECV, H_SEND, H_RECV = range(9)
 RB_SEND, RB_RECV, RA_SEND, RA_RECV, RX_SEND, RX_OWN = range(9, 15)
-STAGES = 15
+A_VIA, B_VIA, RB_VIA, RA_VIA, A_ON, B_ON, RB_ON, RA_ON = range(15, 23)
+STAGES = 23
 
 
 def matmul(left, right):
@@ -47,7 +47,7 @@
 def kernel(
     dims, q_ref, k_ref, v_ref, cluster, owners, pair_list, out_ref,
     x_recv, a_send, a_recv, b_send, b_recv, halo, o_send, o_recv, t_send, t_recv, x_back,
-    pick, pick_t, perm, perm_t,
+    a_via, b_via, rb_via, ra_via, pick, pick_t, perm, perm_t,
     l_a_send, l_a_recv, l_b_send, l_b_recv, l_halo, mask_in, q_mask, k_mask, mask_tile,
     sem, label_sem, out_sem, mask_sem,
 ):
@@ -183,28 +183,74 @@
     lane = iota((slots, HEAD_DIM), 1)
     l_a_send[...] = jnp.where(lane == cl_dev, 1.0 - labels, labels).astype(BF16)
 
-    def first_hop(src, dst, send, recv, par):
+    half, quarter = n_axis // 2, n_axis // 4
+
+    def first_hop(src, dst, send, recv, par, via=None, via_recv=None):
         a, b, c = place(par)
 
-        @pl.loop(1, n_axis)
+        def put(other, target, ref, rows, end):
+            copy_to(
+                src.at[block(other, a_rows)], ref.at[rows], send, end, device(target, b, c, par)
+            ).start()
+
+        opposite = lax.rem(a + half, n_axis)
+        if via is None or not quarter:
+            put(opposite, opposite, dst, block(a, a_rows), recv)
+        else:
+            between = lax.rem(a + n_axis + quarter * (1 - 2 * c), n_axis)
+            put(opposite, between, via, pl.ds(0, a_rows), via_recv)
+
+        @pl.loop(1, half)
         def _(d):
-            other = lax.rem(a + d, n_axis)
-            copy_to(
-                src.at[block(other, a_rows)], dst.at[block(a, a_rows)], send, recv,
-                device(other, b, c, par),
-            ).start()
-
-    def second_hop(src, dst, send, recv, par):
+            for other in (lax.rem(a + d, n_axis), lax.rem(a + n_axis - d, n_axis)):
+                put(other, other, dst, block(a, a_rows), recv)
+
+    def first_on(dst, send, recv, par, via, via_recv):
+        a, b, c = place(par)
+        step = quarter * (1 - 2 * c)
+        wait_bytes(via, via_recv)
+        origin, target = lax.rem(a + n_axis - step, n_axis), lax.rem(a + n_axis + step, n_axis)
+        copy_to(
+            via, dst.at[block(origin, a_rows)], send, recv, device(target, b, c, par)
+        ).start()
+
+    def second_hop(src, dst, send, recv, par, via=None, via_recv=None):
         a, b, c = place(par)
         here = b * CORES + c
 
-        @pl.loop(1, line)
+        def put(other, target, ref, rows, end):
+            copy_to(
+                src.at[block(other, b_rows)], ref.at[rows], send, end,
+                device(a, target // CORES, target % CORES, par),
+            ).start()
+
+        opposite = lax.rem(b + half, n_axis)
+        for end_c in range(CORES):
+            other = opposite * CORES + end_c
+            if via is None or not quarter:
+                put(other, other, dst, block(here, b_rows), recv)
+            else:
+                between = lax.rem(b + n_axis + quarter * (1 - 2 * end_c), n_axis)
+                put(other, between * CORES + end_c, via, block(c, b_rows), via_recv)
+
+        @pl.loop(1, half)
         def _(d):
-            other = lax.rem(here + d, line)
-            copy_to(
-                src.at[block(other, b_rows)], dst.at[block(here, b_rows)], send, recv,
-                device(a, other // CORES, other % CORES, par),
-            ).start()
+            for other in (lax.rem(b + d, n_axis), lax.rem(b + n_axis - d, n_axis)):
+                for end_c in range(CORES):
+                    other_bc = other * CORES + end_c
+                    put(other_bc, other_bc, dst, block(here, b_rows), recv)
+
+        near = b * CORES + 1 - c
+        put(near, near, dst, block(here, b_rows), recv)
+
+    def second_on(dst, send, recv, par, via, via_recv):
+        a, b, c = place(par)
+        step = quarter * (1 - 2 * c)
+        wait_bytes(via, via_recv)
+        origin, target = lax.rem(b + n_axis - step, n_axis), lax.rem(b + n_axis + step, n_axis)
+        copy_to(
+            via, dst.at[block(origin, CORES * b_rows)], send, recv, device(a, target, c, par)
+        ).start()
 
     others_a = pl.ds(0, slots - a_rows)
     others_b = pl.ds(0, slots - b_rows)
@@ -238,14 +284,20 @@
             own_copy(ref, kind, h).wait()
         wait_bytes(x_recv.at[h, pl.ds(0, tokens - rows)], sem.at[X_RECV, h])
         a_send[h] = matmul(pick[...], x_recv[h]).astype(BF16)
-        first_hop(a_send.at[h], a_recv.at[h], sem.at[A_SEND, h], sem.at[A_RECV, h], par)
+        first_hop(
+            a_send.at[h], a_recv.at[h], sem.at[A_SEND, h], sem.at[A_RECV, h], par,
+            a_via.at[h], sem.at[A_VIA, h],
+        )
         keep_a(a_send.at[h], a_recv.at[h], par)
 
     def turn(h):
         par = SWAP * (h % 2)
         wait_bytes(a_recv.at[h, others_a], sem.at[A_RECV, h])
         b_send[h] = matmul(perm[...], a_recv[h]).astype(BF16)
-        second_hop(b_send.at[h], b_recv.at[h], sem.at[B_SEND, h], sem.at[B_RECV, h], par)
+        second_hop(
+            b_send.at[h], b_recv.at[h], sem.at[B_SEND, h], sem.at[B_RECV, h], par,
+            b_via.at[h], sem.at[B_VIA, h],
+        )
         keep_b(b_send.at[h], b_recv.at[h], par)
 
     def share(h):
@@ -291,14 +343,20 @@
                 mixed = mixed + matmul(weights.astype(BF16), value)
             o_send[h, here] = (mixed / total).astype(BF16)
 
-        second_hop(o_send.at[h], o_recv.at[h], sem.at[RB_SEND, h], sem.at[RB_RECV, h], par)
+        second_hop(
+            o_send.at[h], o_recv.at[h], sem.at[RB_SEND, h], sem.at[RB_RECV, h], par,
+            rb_via.at[h], sem.at[RB_VIA, h],
+        )
         keep_b(o_send.at[h], o_recv.at[h], par)
 
     def turn_back(h):
         par = SWAP * (h % 2)
         wait_bytes(o_recv.at[h, others_b], sem.at[RB_RECV, h])
         t_send[h] = matmul(perm_t[...], o_recv[h]).astype(BF16)
-        first_hop(t_send.at[h], t_recv.at[h], sem.at[RA_SEND, h], sem.at[RA_RECV, h], par)
+        first_hop(
+            t_send.at[h], t_recv.at[h], sem.at[RA_SEND, h], sem.at[RA_RECV, h], par,
+            ra_via.at[h], sem.at[RA_VIA, h],
+        )
         keep_a(t_send.at[h], t_recv.at[h], par)
 
     def finish(h):
@@ -351,12 +409,29 @@
                 label = l_b_recv[par] if part == 1 else l_halo[par, part // 2]
                 k_mask[par, part] = matmul(label, shift).astype(BF16)
 
-    stages = (pack, turn, share, attend, turn_back, finish)
-
-    @pl.loop(0, heads + LAG * (len(stages) - 1))
+    def relay(on, dst, send, recv, via, via_recv):
+        def stage(h):
+            on(
+                dst.at[h], sem.at[send, h], sem.at[recv, h], SWAP * (h % 2),
+                via.at[h], sem.at[via_recv, h],
+            )
+
+        return stage
+
+    relays = (
+        (first_on, a_recv, A_ON, A_RECV, a_via, A_VIA),
+        (second_on, b_recv, B_ON, B_RECV, b_via, B_VIA),
+        (second_on, o_recv, RB_ON, RB_RECV, rb_via, RB_VIA),
+        (first_on, t_recv, RA_ON, RA_RECV, ra_via, RA_VIA),
+    )
+    stages = [(0, pack), (2, turn), (4, share), (6, attend), (8, turn_back), (10, finish)]
+    if quarter:
+        stages += [(lag, relay(*r)) for lag, r in zip((1, 3, 7, 9), relays)]
+    stages.sort(key=lambda entry: entry[0])
+
+    @pl.loop(0, heads + 10)
     def _(step):
-        for number, stage in enumerate(stages):
-            lag = LAG * number
+        for lag, stage in stages:
 
             @pl.when((step >= lag) & (step < heads + lag))
             def _():
@@ -381,6 +456,9 @@
         wait_bytes(t_send.at[h, others_a], sem.at[RA_SEND, h])
         wait_bytes(x_back.at[h, pl.ds(0, tokens - rows)], sem.at[RX_SEND, h])
         wait_bytes(x_back.at[h, pl.ds(0, rows)], sem.at[RX_OWN, h])
+        if quarter:
+            for _, _, on, _, via, _ in relays:
+                wait_bytes(via.at[h], sem.at[on, h])
 
     for par in range(pars):
         wait_bytes(l_a_send.at[others_a], label_sem.at[0, par])
@@ -396,7 +474,7 @@
     rows, features = queries.shape
     heads = features // nx // HEAD_DIM
     tokens = rows * nx
-    slots = n_tok * per_pair
+    slots, line = n_tok * per_pair, n_axis * CORES
     tile = 16
 
     pars = 1 + SWAP
@@ -423,6 +501,10 @@
             vmem(heads, slots, thin),
             vmem(heads, slots, thin),
             vmem(heads, tokens, thin),
+            vmem(heads, line * per_pair, wide),
+            vmem(heads, line * per_pair, wide),
+            vmem(heads, line * per_pair, thin),
+            vmem(heads, line * per_pair, thin),
             vmem(slots, tokens),
             vmem(tokens, slots),
             vmem(slots, slots),

time: 128 us -> 136 us (1.062)
  the two profiles are of different devices: /device:TPU:1 before, /device:TPU:12 now
where the time goes in v1:
time: 136 us
  Pallas kernels  134 us (99%)
  local copies, waits for them, and re-layouts  1.77 us (1%)
    pallas_call x1, Pallas kernels, per_device(): pl.pallas_call(functools.partial(kernel, (nx, n_axis, per_pair, heads)),...  134 us

profile of v1, /device:TPU:12, one launch (start us, length us, event | category | flops | bytes accessed | tf_op | source)
XLA Modules:
  0.0 135.7 jit_solution(12666139078165802120)
XLA Ops:
  0.0 133.9 %shard_map.64 = bf16[64,3072]{1,0:T(8,128)(2,1)} custom-call(bf16[64,3072]{1,0:T(8,128)(2,1)} %q_ref.1, bf16[64,3072]{1,0:T(8,128)(2,1)} %k_ref.1, bf16[64,3072]{1,0:T(8,128)(2,1)} %v_ref.1, s32[1,256]{1,0:T(1,128)} %bitcast.3, s32[1,512]{1,0:T(1,128)} %bitcast.2, s32[4,8]{1,0:T(4,128)} %pair_list.1), custom_call_target="tpu_custom_call" | custom-call | tf_op jit(solution)/shard_map/pallas_call | solution.py:486
  133.9 1.8 %copy.8 = bf16[64,3072]{1,0:T(8,128)(2,1)} copy(bf16[64,3072]{1,0:T(8,128)(2,1)} %shard_map.64) | data formatting | bytes 786432

commit v2 on v0

--- a/solution.py
+++ b/solution.py
@@ -12,7 +12,9 @@
 CAP = 128
 CORES = 2
 SWAP = 1
-LAG = 2
+STARTS = (0, 4, 7, 9, 11, 13)
+AHEAD = 2
+LANES = 8
 MASKED = -(2.0**100)
 SCALE_LOG2 = math.log2(math.e) / math.sqrt(HEAD_DIM)
 MESH = pl.DeviceIdType.MESH
@@ -48,7 +50,7 @@
     dims, q_ref, k_ref, v_ref, cluster, owners, pair_list, out_ref,
     x_recv, a_send, a_recv, b_send, b_recv, halo, o_send, o_recv, t_send, t_recv, x_back,
     pick, pick_t, perm, perm_t,
-    l_a_send, l_a_recv, l_b_send, l_b_recv, l_halo, mask_in, q_mask, k_mask, mask_tile,
+    l_a_send, l_a_recv, l_b_send, l_b_recv, l_own, l_halo, mask_in, q_mask, k_mask, mask_tile,
     sem, label_sem, out_sem, mask_sem,
 ):
     nx, n_axis, per_pair, heads = dims
@@ -147,8 +149,7 @@
     ).astype(BF16)
     pl.semaphore_wait(barrier, greeted)
 
-    @pl.loop(0, heads)
-    def _(h):
+    def spread(h):
         for d in range(1, nx):
             other = lax.rem(my_x + d, nx)
             for kind, ref in enumerate((q_ref, k_ref, v_ref)):
@@ -159,6 +160,9 @@
                     sem.at[X_RECV, h],
                     (tok, other),
                 ).start()
+
+    for h in range(min(AHEAD, heads)):
+        spread(h)
 
     if SWAP:
         mask_copy = copy_to(mask_tile, mask_in, mask_sem.at[0], mask_sem.at[1], partner)
@@ -178,50 +182,54 @@
     pick[...] = one_hot(iota((slots, tokens), 0) == pos)
     same = one_hot(iota((tokens, tokens), 0) == iota((tokens, tokens), 1))
     pick_t[...] = matmul_t(same, pick[...]).astype(BF16)
-    lane = iota((HEAD_DIM, tokens), 0)
-    labels = matmul_t(pick[...], one_hot((lane == local_id) | (lane == cl_dev)))
-    lane = iota((slots, HEAD_DIM), 1)
-    l_a_send[...] = jnp.where(lane == cl_dev, 1.0 - labels, labels).astype(BF16)
-
-    def first_hop(src, dst, send, recv, par):
+    lane = iota((HEAD_DIM, tokens), 0) - rank.astype(jnp.int32) * LANES
+    labels = matmul_t(target_hot, one_hot((lane == local_id) | (lane == cl_dev)))
+    lane = iota((n_tok, HEAD_DIM), 1)
+    l_a_send[...] = jnp.where(lane % LANES == cl_dev, 1.0 - labels, labels).astype(BF16)
+
+    def first_hop(src, dst, send, recv, par, size):
         a, b, c = place(par)
 
         @pl.loop(1, n_axis)
         def _(d):
             other = lax.rem(a + d, n_axis)
             copy_to(
-                src.at[block(other, a_rows)], dst.at[block(a, a_rows)], send, recv,
+                src.at[block(other, size)], dst.at[block(a, size)], send, recv,
                 device(other, b, c, par),
             ).start()
 
-    def second_hop(src, dst, send, recv, par):
+    def put(src, dst, send, recv, par, size, other):
         a, b, c = place(par)
-        here = b * CORES + c
+        copy_to(
+            src.at[block(other, size)], dst.at[block(b * CORES + c, size)], send, recv,
+            device(a, other // CORES, other % CORES, par),
+        ).start()
+
+    def second_hop(src, dst, send, recv, par, size):
+        _, b, c = place(par)
 
         @pl.loop(1, line)
         def _(d):
-            other = lax.rem(here + d, line)
-            copy_to(
-                src.at[block(other, b_rows)], dst.at[block(here, b_rows)], send, recv,
-                device(a, other // CORES, other % CORES, par),
-            ).start()
+            put(src, dst, send, recv, par, size, lax.rem(b * CORES + c + d, line))
+
+    def keep_a(src, dst, par, size):
+        a, _, _ = place(par)
+        dst[block(a, size)] = src[block(a, size)]
+
+    def keep_b(src, dst, par, size):
+        _, b, c = place(par)
+        dst[block(b * CORES + c, size)] = src[block(b * CORES + c, size)]
 
     others_a = pl.ds(0, slots - a_rows)
     others_b = pl.ds(0, slots - b_rows)
-
-    def keep_a(src, dst, par):
-        a, _, _ = place(par)
-        dst[block(a, a_rows)] = src[block(a, a_rows)]
-
-    def keep_b(src, dst, par):
-        _, b, c = place(par)
-        dst[block(b * CORES + c, b_rows)] = src[block(b * CORES + c, b_rows)]
+    label_others_a = pl.ds(0, n_tok - line)
+    label_others_b = pl.ds(0, (line - 1) * tile)
 
     for par in range(pars):
         first_hop(
-            l_a_send, l_a_recv.at[par], label_sem.at[0, par], label_sem.at[1, par], par
+            l_a_send, l_a_recv.at[par], label_sem.at[0, par], label_sem.at[1, par], par, line
         )
-        keep_a(l_a_send, l_a_recv.at[par], par)
+        keep_a(l_a_send, l_a_recv.at[par], par, line)
 
     out_row, in_row = iota((slots, slots), 0), iota((slots, slots), 1)
 
@@ -237,16 +245,23 @@
         for kind, ref in enumerate((q_ref, k_ref, v_ref)):
             own_copy(ref, kind, h).wait()
         wait_bytes(x_recv.at[h, pl.ds(0, tokens - rows)], sem.at[X_RECV, h])
+
+        @pl.when(h + AHEAD < heads)
+        def _():
+            spread(h + AHEAD)
+
         a_send[h] = matmul(pick[...], x_recv[h]).astype(BF16)
-        first_hop(a_send.at[h], a_recv.at[h], sem.at[A_SEND, h], sem.at[A_RECV, h], par)
-        keep_a(a_send.at[h], a_recv.at[h], par)
+        first_hop(a_send.at[h], a_recv.at[h], sem.at[A_SEND, h], sem.at[A_RECV, h], par, a_rows)
+        keep_a(a_send.at[h], a_recv.at[h], par, a_rows)
 
     def turn(h):
         par = SWAP * (h % 2)
         wait_bytes(a_recv.at[h, others_a], sem.at[A_RECV, h])
         b_send[h] = matmul(perm[...], a_recv[h]).astype(BF16)
-        second_hop(b_send.at[h], b_recv.at[h], sem.at[B_SEND, h], sem.at[B_RECV, h], par)
-        keep_b(b_send.at[h], b_recv.at[h], par)
+        second_hop(
+            b_send.at[h], b_recv.at[h], sem.at[B_SEND, h], sem.at[B_RECV, h], par, b_rows
+        )
+        keep_b(b_send.at[h], b_recv.at[h], par, b_rows)
 
     def share(h):
         par = SWAP * (h % 2)
@@ -263,8 +278,13 @@
         par = SWAP * (h % 2)
         wait_bytes(halo.at[h], sem.at[H_RECV, h])
 
-        @pl.loop(0, slots // query_rows)
+        _, b, c = place(par)
+        mine = b * CORES + c
+        parts, targets = slots // query_rows, query_rows // b_rows
+
+        @pl.loop(0, parts)
         def _(step):
+            step = lax.rem(step + mine // targets, parts)
             here = block(step, query_rows)
             query = jnp.concatenate(
                 [b_recv[h, here, 0:HEAD_DIM], q_mask[par, here]], axis=1
@@ -291,15 +311,27 @@
                 mixed = mixed + matmul(weights.astype(BF16), value)
             o_send[h, here] = (mixed / total).astype(BF16)
 
-        second_hop(o_send.at[h], o_recv.at[h], sem.at[RB_SEND, h], sem.at[RB_RECV, h], par)
-        keep_b(o_send.at[h], o_recv.at[h], par)
+            @pl.loop(0, targets)
+            def _(d):
+                other = step * targets + lax.rem(mine + d, targets)
+
+                @pl.when(other != mine)
+                def _():
+                    put(
+                        o_send.at[h], o_recv.at[h], sem.at[RB_SEND, h], sem.at[RB_RECV, h],
+                        par, b_rows, other,
+                    )
+
+        keep_b(o_send.at[h], o_recv.at[h], par, b_rows)
 
     def turn_back(h):
         par = SWAP * (h % 2)
         wait_bytes(o_recv.at[h, others_b], sem.at[RB_RECV, h])
         t_send[h] = matmul(perm_t[...], o_recv[h]).astype(BF16)
-        first_hop(t_send.at[h], t_recv.at[h], sem.at[RA_SEND, h], sem.at[RA_RECV, h], par)
-        keep_a(t_send.at[h], t_recv.at[h], par)
+        first_hop(
+            t_send.at[h], t_recv.at[h], sem.at[RA_SEND, h], sem.at[RA_RECV, h], par, a_rows
+        )
+        keep_a(t_send.at[h], t_recv.at[h], par, a_rows)
 
     def finish(h):
         wait_bytes(t_recv.at[h, others_a], sem.at[RA_RECV, h])
@@ -316,47 +348,61 @@
             ).start()
 
     def turn_labels():
+        row, column = iota((line * tile, n_tok), 0), iota((line * tile, n_tok), 1)
+        turned = one_hot((row % tile < n_axis) & (column == row % tile * line + row // tile))
         for par in range(pars):
-            wait_bytes(l_a_recv.at[par, others_a], label_sem.at[1, par])
-            l_b_send[par] = matmul(perm[...], l_a_recv[par]).astype(BF16)
+            wait_bytes(l_a_recv.at[par, label_others_a], label_sem.at[1, par])
+            l_b_send[par] = matmul(turned, l_a_recv[par]).astype(BF16)
             second_hop(
                 l_b_send.at[par], l_b_recv.at[par],
-                label_sem.at[2, par], label_sem.at[3, par], par,
+                label_sem.at[2, par], label_sem.at[3, par], par, tile,
             )
-            keep_b(l_b_send.at[par], l_b_recv.at[par], par)
+            keep_b(l_b_send.at[par], l_b_recv.at[par], par, tile)
 
     def share_labels():
+        row, column = iota((n_tok, line * tile), 0), iota((n_tok, line * tile), 1)
+        dense = one_hot(column == row // n_axis * tile + row % n_axis)
         for par in range(pars):
-            wait_bytes(l_b_recv.at[par, others_b], label_sem.at[3, par])
+            wait_bytes(l_b_recv.at[par, label_others_b], label_sem.at[3, par])
+            l_own[par] = matmul(dense, l_b_recv[par]).astype(BF16)
             for side, step in ((0, 1), (1, -1)):
                 copy_to(
-                    l_b_recv.at[par], l_halo.at[par, side],
+                    l_own.at[par], l_halo.at[par, side],
                     label_sem.at[4, par], label_sem.at[5, par], neighbour(par, step),
                 ).start()
 
     def make_masks():
         row, column = iota((HEAD_DIM, HEAD_DIM), 0), iota((HEAD_DIM, HEAD_DIM), 1)
+        fold = one_hot((row % LANES == column) & (row < per_pair * LANES))
+        owner_row = one_hot(iota((slots, n_tok), 0) // per_pair == iota((slots, n_tok), 1))
+        slot_row, slot_lane = iota((slots, HEAD_DIM), 0), iota((slots, HEAD_DIM), 1)
+        own_lanes = slot_lane // LANES == slot_row % per_pair
+
+        def label_rows(label):
+            spread_rows = jnp.where(own_lanes, matmul(owner_row, label), 0.0).astype(BF16)
+            return matmul(spread_rows, fold).astype(BF16)
+
         if SWAP:
             mask_copy.wait()
         for par in range(pars):
             wait_bytes(l_halo.at[par], label_sem.at[5, par])
             mask = (mask_in if par else mask_tile)[...]
             mask = jnp.concatenate([mask, jnp.zeros((HEAD_DIM - tile, HEAD_DIM), BF16)], axis=0)
-            q_mask[par] = matmul(l_b_recv[par], mask).astype(BF16)
             for part in range(3):
+                label = label_rows(l_own[par] if part == 1 else l_halo[par, part // 2])
                 shift = one_hot(
                     ((row < cl_dev) & (column == row + cl_dev * part))
                     | ((row == cl_dev) & (column == 3 * cl_dev))
                 )
-                label = l_b_recv[par] if part == 1 else l_halo[par, part // 2]
                 k_mask[par, part] = matmul(label, shift).astype(BF16)
-
-    stages = (pack, turn, share, attend, turn_back, finish)
-
-    @pl.loop(0, heads + LAG * (len(stages) - 1))
+                if part == 1:
+                    q_mask[par] = matmul(label, mask).astype(BF16)
+
+    stages = tuple(zip(STARTS, (pack, turn, share, attend, turn_back, finish)))
+
+    @pl.loop(0, heads + STARTS[-1])
     def _(step):
-        for number, stage in enumerate(stages):
-            lag = LAG * number
+        for lag, stage in stages:
 
             @pl.when((step >= lag) & (step < heads + lag))
             def _():
@@ -383,8 +429,8 @@
         wait_bytes(x_back.at[h, pl.ds(0, rows)], sem.at[RX_OWN, h])
 
     for par in range(pars):
-        wait_bytes(l_a_send.at[others_a], label_sem.at[0, par])
-        wait_bytes(l_b_send.at[par, others_b], label_sem.at[2, par])
+        wait_bytes(l_a_send.at[label_others_a], label_sem.at[0, par])
+        wait_bytes(l_b_send.at[par, label_others_b], label_sem.at[2, par])
         wait_bytes(l_halo.at[par], label_sem.at[4, par])
 
 
@@ -396,7 +442,7 @@
     rows, features = queries.shape
     heads = features // nx // HEAD_DIM
     tokens = rows * nx
-    slots = n_tok * per_pair
+    slots, line = n_tok * per_pair, n_axis * CORES
     tile = 16
 
     pars = 1 + SWAP
@@ -427,11 +473,12 @@
             vmem(tokens, slots),
             vmem(slots, slots),
             vmem(slots, slots),
-            vmem(slots, thin),
-            vmem(pars, slots, thin),
-            vmem(pars, slots, thin),
-            vmem(pars, slots, thin),
-            vmem(pars, 2, slots, thin),
+            vmem(n_tok, thin),
+            vmem(pars, n_tok, thin),
+            vmem(pars, line * tile, thin),
+            vmem(pars, line * tile, thin),
+            vmem(pars, n_tok, thin),
+            vmem(pars, 2, n_tok, thin),
             vmem(tile, thin),
             vmem(pars, slots, thin),
             vmem(pars, 3, slots, thin),

time: 128 us -> 131 us (1.023)
  the two profiles are of different devices: /device:TPU:1 before, /device:TPU:64 now
where the time goes in v2:
time: 131 us
  Pallas kernels  129 us (98%)
  local copies, waits for them, and re-layouts  1.77 us (1%)
    pallas_call x1, Pallas kernels, per_device(): pl.pallas_call(functools.partial(kernel, (nx, n_axis, per_pair, heads)),...  129 us

profile of v2, /device:TPU:64, one launch (start us, length us, event | category | flops | bytes accessed | tf_op | source)
XLA Modules:
  0.0 130.6 jit_solution(5137969224507656272)
XLA Ops:
  0.0 128.8 %shard_map.64 = bf16[64,3072]{1,0:T(8,128)(2,1)} custom-call(bf16[64,3072]{1,0:T(8,128)(2,1)} %q_ref.1, bf16[64,3072]{1,0:T(8,128)(2,1)} %k_ref.1, bf16[64,3072]{1,0:T(8,128)(2,1)} %v_ref.1, s32[1,256]{1,0:T(1,128)} %bitcast.3, s32[1,512]{1,0:T(1,128)} %bitcast.2, s32[4,8]{1,0:T(4,128)} %pair_list.1), custom_call_target="tpu_custom_call" | custom-call | tf_op jit(solution)/shard_map/pallas_call | solution.py:454
  128.8 1.8 %copy.8 = bf16[64,3072]{1,0:T(8,128)(2,1)} copy(bf16[64,3072]{1,0:T(8,128)(2,1)} %shard_map.64) | data formatting | bytes 786432

commit v3 on v2

--- a/solution.py
+++ b/solution.py
@@ -187,12 +187,17 @@
     lane = iota((n_tok, HEAD_DIM), 1)
     l_a_send[...] = jnp.where(lane % LANES == cl_dev, 1.0 - labels, labels).astype(BF16)
 
+    half = n_axis // 2
+
+    def both_ways(here):
+        far = [lax.rem(here + half, n_axis)]
+        for d in range(half - 1, 0, -1):
+            far += [lax.rem(here + d, n_axis), lax.rem(here + n_axis - d, n_axis)]
+        return far
+
     def first_hop(src, dst, send, recv, par, size):
         a, b, c = place(par)
-
-        @pl.loop(1, n_axis)
-        def _(d):
-            other = lax.rem(a + d, n_axis)
+        for other in both_ways(a):
             copy_to(
                 src.at[block(other, size)], dst.at[block(a, size)], send, recv,
                 device(other, b, c, par),
@@ -207,10 +212,10 @@
 
     def second_hop(src, dst, send, recv, par, size):
         _, b, c = place(par)
-
-        @pl.loop(1, line)
-        def _(d):
-            put(src, dst, send, recv, par, size, lax.rem(b * CORES + c + d, line))
+        for other in both_ways(b):
+            for end_c in range(CORES):
+                put(src, dst, send, recv, par, size, other * CORES + end_c)
+        put(src, dst, send, recv, par, size, b * CORES + 1 - c)
 
     def keep_a(src, dst, par, size):
         a, _, _ = place(par)
@@ -278,13 +283,8 @@
         par = SWAP * (h % 2)
         wait_bytes(halo.at[h], sem.at[H_RECV, h])
 
-        _, b, c = place(par)
-        mine = b * CORES + c
-        parts, targets = slots // query_rows, query_rows // b_rows
-
-        @pl.loop(0, parts)
+        @pl.loop(0, slots // query_rows)
         def _(step):
-            step = lax.rem(step + mine // targets, parts)
             here = block(step, query_rows)
             query = jnp.concatenate(
                 [b_recv[h, here, 0:HEAD_DIM], q_mask[par, here]], axis=1
@@ -311,17 +311,7 @@
                 mixed = mixed + matmul(weights.astype(BF16), value)
             o_send[h, here] = (mixed / total).astype(BF16)
 
-            @pl.loop(0, targets)
-            def _(d):
-                other = step * targets + lax.rem(mine + d, targets)
-
-                @pl.when(other != mine)
-                def _():
-                    put(
-                        o_send.at[h], o_recv.at[h], sem.at[RB_SEND, h], sem.at[RB_RECV, h],
-                        par, b_rows, other,
-                    )
-
+        second_hop(o_send.at[h], o_recv.at[h], sem.at[RB_SEND, h], sem.at[RB_RECV, h], par, b_rows)
         keep_b(o_send.at[h], o_recv.at[h], par, b_rows)
 
     def turn_back(h):

time: 131 us -> 130 us (level)
  the two profiles are of different devices: /device:TPU:64 before, /device:TPU:1 now
where the time goes in v3:
time: 130 us
  Pallas kernels  128 us (98%)
  local copies, waits for them, and re-layouts  1.77 us (1%)
    pallas_call x1, Pallas kernels, per_device(): pl.pallas_call(functools.partial(kernel, (nx, n_axis, per_pair, heads)),...  128 us

profile of v3, /device:TPU:1, one launch (start us, length us, event | category | flops | bytes accessed | tf_op | source)
XLA Modules:
  0.0 129.7 jit_solution(18036682976575177304)
XLA Ops:
  0.0 127.9 %shard_map.64 = bf16[64,3072]{1,0:T(8,128)(2,1)} custom-call(bf16[64,3072]{1,0:T(8,128)(2,1)} %q_ref.1, bf16[64,3072]{1,0:T(8,128)(2,1)} %k_ref.1, bf16[64,3072]{1,0:T(8,128)(2,1)} %v_ref.1, s32[1,256]{1,0:T(1,128)} %bitcast.3, s32[1,512]{1,0:T(1,128)} %bitcast.2, s32[4,8]{1,0:T(4,128)} %pair_list.1), custom_call_target="tpu_custom_call" | custom-call | tf_op jit(solution)/shard_map/pallas_call | solution.py:444
  128.0 1.8 %copy.8 = bf16[64,3072]{1,0:T(8,128)(2,1)} copy(bf16[64,3072]{1,0:T(8,128)(2,1)} %shard_map.64) | data formatting | bytes 786432

commit v4 on v2

v4 whole, which is shorter than its diff:
```python
import functools
import math

import jax
import jax.numpy as jnp
from jax import lax
from jax.experimental import pallas as pl
from jax.experimental.pallas import tpu as pltpu
from jax.sharding import PartitionSpec as P

HEAD_DIM = 128
CAP = 128
CORES = 2
TILE = 16
LANES = 8
AHEAD = 2
STEP = 1
MASKED = -(2.0**100)
SCALE_LOG2 = math.log2(math.e) / math.sqrt(HEAD_DIM)
MESH = pl.DeviceIdType.MESH
F32 = jnp.float32
BF16 = jnp.bfloat16

X_OWN, X_SEND, X_RECV, A_SEND, A_RECV, B_SEND, B_NEAR, B_RECV, H_SEND, H_RECV = range(10)
RB_SEND, RB_RECV, RA_SEND, RA_RECV, RX_SEND, RX_OWN = range(10, 16)
STAGES = 16


def matmul(left, right):
    return jnp.dot(left, right, preferred_element_type=F32)


def matmul_t(left, right):
    return lax.dot_general(left, right, (((1,), (1,)), ((), ())), preferred_element_type=F32)


def iota(shape, dim):
    return lax.broadcasted_iota(jnp.int32, shape, dim)


def one_hot(condition):
    return jnp.where(condition, 1.0, 0.0).astype(BF16)


def wait_bytes(ref, sem):
    pltpu.make_async_copy(ref, ref, sem).wait()


def kernel(
    dims, q_ref, k_ref, v_ref, cluster, owners, pair_list, out_ref,
    x_recv, a_send, a_recv, b_send, work, o_send, o_recv, t_send, t_recv, x_back,
    pick, pick_t, perm, perm_t, scores, peak, total, mixed,
    l_a_send, l_a_recv, l_b_send, l_b_recv, labels, mask_tile, mask_in, q_mask, k_mask,
    sem, label_sem, mask_sem, out_sem,
):
    nx, n_axis, per_pair, heads = dims
    rows = q_ref.shape[0]
    tokens = nx * rows
    width = heads * HEAD_DIM
    line = n_axis * CORES
    n_tok = n_axis * line
    slots = n_tok * per_pair
    a_rows = line * per_pair
    b_rows = n_axis * per_pair
    mine = heads // CORES
    sides = CORES + 2
    cl_dev, pairs = pair_list.shape
    invalid = sides * cl_dev
    my_x = lax.axis_index("head")
    tok = lax.axis_index("tok")
    z, y, core = tok // line, (tok // CORES) % n_axis, tok % CORES

    def place(par):
        return z + par * (y - z), y + par * (z - y)

    def device(a, b, c, par):
        return ((a + par * (b - a)) * line + (b + par * (a - b)) * CORES + c, my_x)

    def next_chip(step):
        a, b = place(core)
        chip = lax.rem(a * n_axis + b + n_axis * n_axis + step, n_axis * n_axis)
        return device(chip // n_axis, chip % n_axis, core, core)

    def copy_to(src, dst, send, recv, target):
        pltpu.make_async_remote_copy(
            src_ref=src, dst_ref=dst, send_sem=send, recv_sem=recv,
            device_id=target, device_id_type=MESH,
        ).start()

    def lanes(start, size):
        return pl.ds(pl.multiple_of(start, HEAD_DIM), size)

    def block(index, size):
        return pl.ds(pl.multiple_of(index * size, size), size)

    barrier = pltpu.get_barrier_semaphore()

    def greet(target):
        pl.semaphore_signal(barrier, inc=1, device_id=target, device_id_type=MESH)

    @pl.loop(1, nx)
    def _(d):
        greet((tok, lax.rem(my_x + d, nx)))

    @pl.loop(1, line)
    def _(d):
        greet((z * line + lax.rem(y * CORES + core + d, line), my_x))

    @pl.loop(1, n_axis)
    def _(d):
        for c in range(CORES):
            greet(((lax.rem(z + d, n_axis) * n_axis + y) * CORES + c, my_x))

    greet(next_chip(1))
    greet(next_chip(-1))
    @pl.when(y != z)
    def _():
        for c in range(CORES):
            greet(((y * n_axis + z) * CORES + c, my_x))

    @pl.when(y == z)
    def _():
        for c in range(CORES):
            greet((tok + 1 - 2 * core, my_x))

    greeted = (nx - 1) + (line - 1) + (n_axis - 1) * CORES + 2 + CORES

    def own_copy(ref, kind, h):
        return pltpu.make_async_copy(
            ref.at[:, lanes(my_x * width + h * HEAD_DIM, HEAD_DIM)],
            x_recv.at[h, block(my_x, rows), pl.ds(kind * HEAD_DIM, HEAD_DIM)],
            sem.at[X_OWN, h],
        )

    @pl.loop(0, heads)
    def _(h):
        for kind, ref in enumerate((q_ref, k_ref, v_ref)):
            own_copy(ref, kind, h).start()

    pair_local = pair_list[...] - (tok - core - 1) * cl_dev
    lane = iota((cl_dev, HEAD_DIM), 1)
    allowed = lane > invalid
    for j in range(pairs):
        allowed = allowed | (pair_local[:, j : j + 1] == lane)
    mask_tile[...] = jnp.concatenate(
        [jnp.where(allowed, 0.0, MASKED), jnp.zeros((TILE - cl_dev, HEAD_DIM), F32)], axis=0
    ).astype(BF16)

    pl.semaphore_wait(barrier, greeted)

    def spread(h):
        @pl.loop(1, nx)
        def _(d):
            other = lax.rem(my_x + d, nx)
            for kind, ref in enumerate((q_ref, k_ref, v_ref)):
                copy_to(
                    ref.at[:, lanes(other * width + h * HEAD_DIM, HEAD_DIM)],
                    x_recv.at[h, block(my_x, rows), pl.ds(kind * HEAD_DIM, HEAD_DIM)],
                    sem.at[X_SEND, h],
                    sem.at[X_RECV, h],
                    (tok, other),
                )

    @pl.loop(0, min(AHEAD, heads))
    def _(h):
        spread(h)

    keepers = [(z * n_axis + y) * CORES, (y * n_axis + z) * CORES + 1]
    for end, keeper in enumerate(keepers):

        @pl.when(tok == keeper)
        def _():
            pltpu.make_async_copy(
                mask_tile, mask_in.at[core], mask_sem.at[CORES + core]
            ).start()

        @pl.when(tok != keeper)
        def _():
            copy_to(
                mask_tile, mask_in.at[core], mask_sem.at[end], mask_sem.at[CORES + core],
                (keeper, my_x),
            )

    clusters = owners.shape[1]
    cluster_hot = one_hot(iota((clusters, tokens), 0) == cluster[...])
    table = jnp.where(
        iota((TILE, clusters), 0) == 0, owners[...] // cl_dev, owners[...] % cl_dev
    )
    found = matmul(table.astype(F32).astype(BF16), cluster_hot).astype(jnp.int32)
    target, local_id = found[0:1], found[1:2]
    target_hot = one_hot(iota((n_tok, tokens), 0) == target)
    earlier = one_hot(iota((tokens, tokens), 0) < iota((tokens, tokens), 1))
    rank = jnp.sum(matmul(target_hot, earlier) * target_hot.astype(F32), axis=0, keepdims=True)
    rank = rank.astype(jnp.int32)
    send_row = target * per_pair + rank
    chunk = min(128, tokens)

    @pl.loop(0, slots // chunk)
    def _(i):
        pick[block(i, chunk)] = one_hot(iota((chunk, tokens), 0) + i * chunk == send_row)

    lane = iota((HEAD_DIM, tokens), 0) - rank * LANES
    filled = matmul_t(target_hot, one_hot((lane == local_id) | (lane == cl_dev)))
    lane = iota((n_tok, HEAD_DIM), 1)
    l_a_send[...] = jnp.where(lane % LANES == cl_dev, 1.0 - filled, filled).astype(BF16)

    def first_hop(src, dst, send, recv, par, size):
        a, b = place(par)
        pltpu.make_async_copy(src.at[block(a, size)], dst.at[block(a, size)], recv).start()

        @pl.loop(1, n_axis)
        def _(d):
            other = lax.rem(a + d, n_axis)
            copy_to(
                src.at[block(other, size)], dst.at[block(a, size)], send, recv,
                device(other, b, core, par),
            )

    def second_hop(src_at, dst, send, near, recv, par):
        a, b = place(par)

        @pl.when(core == par)
        def _():
            pltpu.make_async_copy(src_at(b), dst, recv).start()

        @pl.when(core != par)
        def _():
            copy_to(src_at(b), dst, near, recv, device(a, b, par, par))

        @pl.loop(1, n_axis)
        def _(d):
            other = lax.rem(b + d, n_axis)
            copy_to(src_at(other), dst, send, recv, device(a, other, par, par))

    def source(par):
        _, b = place(par)
        return b * CORES + core

    others_a = pl.ds(0, slots - a_rows)
    others_b = pl.ds(0, b_rows * (n_axis - 1))
    label_others = pl.ds(0, n_tok - line)

    for par in range(CORES):
        first_hop(
            l_a_send, l_a_recv.at[par], label_sem.at[0, par], label_sem.at[1, par], par, line
        )

    def pack(h):
        for kind, ref in enumerate((q_ref, k_ref, v_ref)):
            own_copy(ref, kind, h).wait()
        wait_bytes(x_recv.at[h, pl.ds(0, tokens - rows)], sem.at[X_RECV, h])

        @pl.when(h + AHEAD < heads)
        def _():
            spread(h + AHEAD)

        @pl.loop(0, 2)
        def _(i):
            part = block(i, slots // 2)
            a_send[h, part] = matmul(pick[part], x_recv[h]).astype(BF16)

        first_hop(a_send.at[h], a_recv.at[h], sem.at[A_SEND, h], sem.at[A_RECV, h], h % 2, a_rows)

    def turn(h):
        par = h % 2
        wait_bytes(a_recv.at[h], sem.at[A_RECV, h])

        @pl.loop(0, CORES)
        def _(i):
            b_send[h, i] = matmul(perm[i], a_recv[h]).astype(BF16)

        second_hop(
            lambda other: b_send.at[h, :, block(other, b_rows)],
            work.at[h // 2, pl.ds(1, CORES), block(source(par), b_rows)],
            sem.at[B_SEND, h], sem.at[B_NEAR, h], sem.at[B_RECV, h // 2], par,
        )

    def share(k):
        wait_bytes(work.at[k, pl.ds(1, CORES)], sem.at[B_RECV, k])
        for step, src, dst in ((-1, 1, CORES + 1), (1, CORES, 0)):
            copy_to(
                work.at[k, src, :, pl.ds(HEAD_DIM, 2 * HEAD_DIM)],
                work.at[k, dst, :, pl.ds(HEAD_DIM, 2 * HEAD_DIM)],
                sem.at[H_SEND, k], sem.at[H_RECV, k], next_chip(step),
            )

    two_sides = (pl.ds(0, 2), slice(None), pl.ds(HEAD_DIM, 2 * HEAD_DIM))
    tiles = slots // HEAD_DIM if slots >= HEAD_DIM else 1
    lane_step = min(slots, HEAD_DIM)

    def attend(k):
        wait_bytes(work.at[(k, *two_sides)], sem.at[H_RECV, k])

        @pl.loop(0, CORES)
        def _(i):
            peak[...] = jnp.full((slots, lane_step), -jnp.inf, F32)

            @pl.loop(0, 3)
            def _(part):
                query = jnp.concatenate([work[k, i + 1, :, 0:HEAD_DIM], q_mask[i]], axis=1)
                key = jnp.concatenate(
                    [work[k, i + part, :, HEAD_DIM : 2 * HEAD_DIM], k_mask[i + part]], axis=1
                )
                found = matmul_t(query, key)
                scores[part] = found
                peak[...] = functools.reduce(
                    jnp.maximum,
                    [found[:, t * lane_step : (t + 1) * lane_step] for t in range(tiles)],
                    peak[...],
                )

            row_max = jnp.max(peak[...], axis=1, keepdims=True)
            peak[...] = jnp.broadcast_to(row_max, (slots, lane_step))
            total[...] = jnp.zeros((slots, lane_step), F32)
            mixed[...] = jnp.zeros((slots, HEAD_DIM), F32)

            @pl.loop(0, 3)
            def _(part):
                row_max = peak[...]
                weights = [
                    jnp.exp2(
                        (scores[part, :, t * lane_step : (t + 1) * lane_step] - row_max)
                        * SCALE_LOG2
                    )
                    for t in range(tiles)
                ]
                total[...] += functools.reduce(jnp.add, weights)
                rounded = jnp.concatenate([w.astype(BF16) for w in weights], axis=1)
                mixed[...] += matmul(rounded, work[k, i + part, :, 2 * HEAD_DIM : 3 * HEAD_DIM])

            row_total = jnp.sum(total[...], axis=1, keepdims=True)
            o_send[k, i] = (mixed[...] / row_total).astype(BF16)

        h = CORES * k + core
        a, b = place(core)
        here = b * CORES + core
        dst = o_recv.at[h, :, block(b, b_rows)]

        def src(other):
            return o_send.at[k, :, block(other, b_rows)]

        pltpu.make_async_copy(src(here), dst, sem.at[RB_RECV, h]).start()

        @pl.loop(1, line)
        def _(d):
            other = lax.rem(here + d, line)
            copy_to(
                src(other), dst, sem.at[RB_SEND, k], sem.at[RB_RECV, h],
                device(a, other // CORES, other % CORES, core),
            )

    def turn_back(h):
        wait_bytes(o_recv.at[h], sem.at[RB_RECV, h])
        t_send[h] = matmul(perm_t[...], o_recv[h].reshape(slots, HEAD_DIM)).astype(BF16)
        first_hop(
            t_send.at[h], t_recv.at[h], sem.at[RA_SEND, h], sem.at[RA_RECV, h], h % 2, a_rows
        )

    def finish(h):
        wait_bytes(t_recv.at[h], sem.at[RA_RECV, h])
        x_back[h] = matmul(pick_t[...], t_recv[h]).astype(BF16)
        column = lanes(my_x * width + h * HEAD_DIM, HEAD_DIM)
        pltpu.make_async_copy(
            x_back.at[h, block(my_x, rows)], out_ref.at[:, column], sem.at[RX_OWN, h]
        ).start()

        @pl.loop(1, nx)
        def _(d):
            other = lax.rem(my_x + d, nx)
            copy_to(
                x_back.at[h, block(other, rows)], out_ref.at[:, column],
                sem.at[RX_SEND, h], out_sem, (tok, other),
            )

    def make_perms():
        half = slots // CORES

        def source_of(row, i):
            r, a, b = row % per_pair, (row // per_pair) % n_axis, row // b_rows
            return a * a_rows + b * (CORES * per_pair) + i * per_pair + r

        for i in range(CORES):
            perm[i] = one_hot(source_of(iota((half, slots), 0), i) == iota((half, slots), 1))

        @pl.loop(0, slots // chunk)
        def _(part):
            row, column = iota((chunk, slots), 0) + part * chunk, iota((chunk, slots), 1)
            perm_t[block(part, chunk)] = one_hot(
                source_of(column % half, column // half) == row
            )

        same = one_hot(iota((tokens, tokens), 0) == iota((tokens, tokens), 1))
        pick_t[...] = matmul_t(same, pick[...]).astype(BF16)

    def turn_labels():
        row, column = iota((n_tok, n_tok), 0), iota((n_tok, n_tok), 1)
        start = (row // CORES) % n_axis * line + row // line * CORES + row % CORES
        turned = one_hot(start == column)
        for par in range(CORES):
            wait_bytes(l_a_recv.at[par], label_sem.at[1, par])
            l_b_send[par] = matmul(turned, l_a_recv[par]).astype(BF16)
            second_hop(
                lambda other: l_b_send.at[par, block(other, line)],
                l_b_recv.at[block(source(par), line)],
                label_sem.at[2, par], label_sem.at[3, par], label_sem.at[4, 0], par,
            )

    def share_labels():
        wait_bytes(l_b_recv, label_sem.at[4, 0])
        shape = (n_tok, line * line)
        row, column = iota(shape, 0), iota(shape, 1)
        start = row // n_axis * line + row % n_axis * CORES
        for i in range(CORES):
            labels[i + 1] = matmul(one_hot(start + i == column), l_b_recv[...]).astype(BF16)
        for step, src, dst in ((-1, 1, CORES + 1), (1, CORES, 0)):
            copy_to(
                labels.at[src], labels.at[dst], label_sem.at[5, 0], label_sem.at[5, 1],
                next_chip(step),
            )

    def make_masks():
        wait_bytes(labels.at[pl.ds(0, 2)], label_sem.at[5, 1])
        for c in range(CORES):
            wait_bytes(mask_in.at[c], mask_sem.at[CORES + c])
        row, column = iota((HEAD_DIM, HEAD_DIM), 0), iota((HEAD_DIM, HEAD_DIM), 1)
        fold = one_hot((row % LANES == column) & (row < per_pair * LANES))
        owner_row = one_hot(iota((slots, n_tok), 0) // per_pair == iota((slots, n_tok), 1))
        shape = (slots, HEAD_DIM)
        own_lanes = iota(shape, 1) // LANES == iota(shape, 0) % per_pair
        rest = jnp.zeros((HEAD_DIM - TILE, HEAD_DIM), BF16)

        @pl.loop(0, sides)
        def _(side):
            spaced = jnp.where(own_lanes, matmul(owner_row, labels[side]), 0.0).astype(BF16)
            label = matmul(spaced, fold).astype(BF16)
            shift = one_hot(
                ((row < cl_dev) & (column == row + cl_dev * side))
                | ((row == cl_dev) & (column == invalid))
            )
            k_mask[side] = matmul(label, shift).astype(BF16)

            @pl.when((side >= 1) & (side <= CORES))
            def _():
                mask = jnp.concatenate([mask_in[side - 1], rest], axis=0)
                q_mask[side - 1] = matmul(label, mask).astype(BF16)

    def both(stage):
        def pair(k):
            @pl.loop(CORES * k, CORES * k + CORES)
            def _(h):
                stage(h)

        return pair

    stages = (both(pack), both(turn), share, attend, both(turn_back), both(finish))

    @pl.loop(0, mine + STEP * (len(stages) - 1))
    def _(step):
        for number, stage in enumerate(stages):
            lag = STEP * number

            @pl.when((step >= lag) & (step < mine + lag))
            def _():
                stage(step - lag)

            if number == 0:

                @pl.when(step == 0)
                def _():
                    make_perms()
                    turn_labels()

        @pl.when(step == 1)
        def _():
            share_labels()

        @pl.when(step == 2)
        def _():
            make_masks()

    wait_bytes(out_ref.at[:, pl.ds(0, (nx - 1) * width)], out_sem)

    @pl.loop(0, heads)
    def _(h):
        wait_bytes(x_recv.at[h, pl.ds(0, tokens - rows)], sem.at[X_SEND, h])
        wait_bytes(a_send.at[h, others_a], sem.at[A_SEND, h])
        wait_bytes(b_send.at[h, :, others_b], sem.at[B_SEND, h])
        wait_bytes(t_send.at[h, others_a], sem.at[RA_SEND, h])
        wait_bytes(x_back.at[h, pl.ds(0, tokens - rows)], sem.at[RX_SEND, h])
        wait_bytes(x_back.at[h, pl.ds(0, rows)], sem.at[RX_OWN, h])

        @pl.when(core != h % 2)
        def _():
            wait_bytes(b_send.at[h, :, pl.ds(0, b_rows)], sem.at[B_NEAR, h])

    @pl.loop(0, mine)
    def _(k):
        wait_bytes(work.at[(k, *two_sides)], sem.at[H_SEND, k])
        wait_bytes(o_send.at[k, :, pl.ds(0, (line - 1) * b_rows)], sem.at[RB_SEND, k])

    for par in range(CORES):
        wait_bytes(l_a_send.at[label_others], label_sem.at[0, par])
        wait_bytes(l_b_send.at[par, label_others], label_sem.at[2, par])

        @pl.when(core != par)
        def _():
            wait_bytes(l_b_send.at[par, pl.ds(0, line)], label_sem.at[3, par])

        @pl.when(tok != keepers[par])
        def _():
            wait_bytes(mask_tile, mask_sem.at[par])

    wait_bytes(labels.at[pl.ds(0, 2)], label_sem.at[5, 0])


def per_device(queries, key_rows, values, cluster, owners, pair_list):
    nx, n_tok = lax.axis_size("head"), lax.axis_size("tok")
    n_axis = math.isqrt(n_tok // CORES)
    cl_dev = pair_list.shape[0]
    per_pair = CAP * cl_dev // n_tok
    rows, features = queries.shape
    heads = features // nx // HEAD_DIM
    tokens = rows * nx
    slots, line = n_tok * per_pair, n_axis * CORES
    mine, sides, half = heads // CORES, CORES + 2, slots // CORES
    wide, thin = 3 * HEAD_DIM, HEAD_DIM
    lane_step = min(slots, HEAD_DIM)

    def vmem(*shape, dtype=BF16):
        return pltpu.VMEM(shape, dtype)

    return pl.pallas_call(
        functools.partial(kernel, (nx, n_axis, per_pair, heads)),
        out_shape=jax.ShapeDtypeStruct((rows, features), BF16),
        in_specs=[pl.BlockSpec(memory_space=pltpu.HBM)] * 3
        + [pl.BlockSpec(memory_space=pltpu.VMEM)] * 3,
        out_specs=pl.BlockSpec(memory_space=pltpu.HBM),
        scratch_shapes=[
            vmem(heads, tokens, wide),
            vmem(heads, slots, wide),
            vmem(heads, slots, wide),
            vmem(heads, CORES, half, wide),
            vmem(mine, sides, slots, wide),
            vmem(mine, CORES, slots, thin),
            vmem(heads, CORES, half, thin),
            vmem(heads, slots, thin),
            vmem(heads, slots, thin),
            vmem(heads, tokens, thin),
            vmem(slots, tokens),
            vmem(tokens, slots),
            vmem(CORES, half, slots),
            vmem(slots, slots),
            vmem(3, slots, slots, dtype=F32),
            vmem(slots, lane_step, dtype=F32),
            vmem(slots, lane_step, dtype=F32),
            vmem(slots, thin, dtype=F32),
            vmem(n_tok, thin),
            vmem(CORES, n_tok, thin),
            vmem(CORES, n_tok, thin),
            vmem(line * line, thin),
            vmem(sides, n_tok, thin),
            vmem(TILE, thin),
            vmem(CORES, TILE, thin),
            vmem(CORES, slots, thin),
            vmem(sides, slots, thin),
            pltpu.SemaphoreType.DMA((STAGES, heads)),
            pltpu.SemaphoreType.DMA((6, 2)),
            pltpu.SemaphoreType.DMA((2 * CORES,)),
            pltpu.SemaphoreType.DMA,
        ],
        compiler_params=pltpu.CompilerParams(
            collective_id=0, has_side_effects=True, vmem_limit_bytes=60 * 2**20
        ),
    )(queries, key_rows, values, cluster[None, :], owners[None, :], pair_list)


def solution(mesh):
    return jax.shard_map(
        per_device,
        mesh=mesh,
        in_specs=(
            P(("tok", "head"), None),
            P(("tok", "head"), None),
            P(("tok", "head"), None),
            P("tok"),
            P(),
            P("tok", None),
        ),
        out_specs=P(("tok", "head"), None),
        check_vma=False,
    )
```

time: 131 us -> 125 us (0.954)
  the two profiles are of different devices: /device:TPU:64 before, /device:TPU:1 now
where the time goes in v4:
time: 125 us
  Pallas kernels  123 us (98%)
  local copies, waits for them, and re-layouts  1.77 us (1%)
    pallas_call x1, Pallas kernels, per_device(): pl.pallas_call(functools.partial(kernel, (nx, n_axis, per_pair, heads)),...  123 us

profile of v4, /device:TPU:1, one launch (start us, length us, event | category | flops | bytes accessed | tf_op | source)
XLA Modules:
  0.0 124.6 jit_solution(9401613467013070514)
XLA Ops:
  0.0 122.9 %shard_map.64 = bf16[64,3072]{1,0:T(8,128)(2,1)} custom-call(bf16[64,3072]{1,0:T(8,128)(2,1)} %q_ref.1, bf16[64,3072]{1,0:T(8,128)(2,1)} %k_ref.1, bf16[64,3072]{1,0:T(8,128)(2,1)} %v_ref.1, s32[1,256]{1,0:T(1,128)} %bitcast.3, s32[1,512]{1,0:T(1,128)} %bitcast.2, s32[4,8]{1,0:T(4,128)} %pair_list.1), custom_call_target="tpu_custom_call" | custom-call | tf_op jit(solution)/shard_map/pallas_call | solution.py:532
  122.9 1.8 %copy.8 = bf16[64,3072]{1,0:T(8,128)(2,1)} copy(bf16[64,3072]{1,0:T(8,128)(2,1)} %shard_map.64) | data formatting | bytes 786432

commit v5 on v4

--- a/solution.py
+++ b/solution.py
@@ -132,20 +132,6 @@
             sem.at[X_OWN, h],
         )
 
-    @pl.loop(0, heads)
-    def _(h):
-        for kind, ref in enumerate((q_ref, k_ref, v_ref)):
-            own_copy(ref, kind, h).start()
-
-    pair_local = pair_list[...] - (tok - core - 1) * cl_dev
-    lane = iota((cl_dev, HEAD_DIM), 1)
-    allowed = lane > invalid
-    for j in range(pairs):
-        allowed = allowed | (pair_local[:, j : j + 1] == lane)
-    mask_tile[...] = jnp.concatenate(
-        [jnp.where(allowed, 0.0, MASKED), jnp.zeros((TILE - cl_dev, HEAD_DIM), F32)], axis=0
-    ).astype(BF16)
-
     pl.semaphore_wait(barrier, greeted)
 
     def spread(h):
@@ -164,6 +150,20 @@
     @pl.loop(0, min(AHEAD, heads))
     def _(h):
         spread(h)
+
+    @pl.loop(0, heads)
+    def _(h):
+        for kind, ref in enumerate((q_ref, k_ref, v_ref)):
+            own_copy(ref, kind, h).start()
+
+    pair_local = pair_list[...] - (tok - core - 1) * cl_dev
+    lane = iota((cl_dev, HEAD_DIM), 1)
+    allowed = lane > invalid
+    for j in range(pairs):
+        allowed = allowed | (pair_local[:, j : j + 1] == lane)
+    mask_tile[...] = jnp.concatenate(
+        [jnp.where(allowed, 0.0, MASKED), jnp.zeros((TILE - cl_dev, HEAD_DIM), F32)], axis=0
+    ).astype(BF16)
 
     keepers = [(z * n_axis + y) * CORES, (y * n_axis + z) * CORES + 1]
     for end, keeper in enumerate(keepers):
@@ -289,37 +289,42 @@
     lane_step = min(slots, HEAD_DIM)
 
     def attend(k):
-        wait_bytes(work.at[(k, *two_sides)], sem.at[H_RECV, k])
+        peak[...] = jnp.full((CORES, slots, lane_step), -jnp.inf, F32)
+
+        @pl.loop(0, 3 * CORES)
+        def _(n):
+            i = (n // 2) % 2 + n // 5
+            part = 1 - i + n % 2 + (n // 4) * (2 * i - 1)
+
+            @pl.when(n == 4)
+            def _():
+                wait_bytes(work.at[(k, *two_sides)], sem.at[H_RECV, k])
+
+            query = jnp.concatenate([work[k, i + 1, :, 0:HEAD_DIM], q_mask[i]], axis=1)
+            key = jnp.concatenate(
+                [work[k, i + part, :, HEAD_DIM : 2 * HEAD_DIM], k_mask[i + part]], axis=1
+            )
+            found = matmul_t(query, key)
+            scores[i, part] = found
+            peak[i] = functools.reduce(
+                jnp.maximum,
+                [found[:, t * lane_step : (t + 1) * lane_step] for t in range(tiles)],
+                peak[i],
+            )
 
         @pl.loop(0, CORES)
         def _(i):
-            peak[...] = jnp.full((slots, lane_step), -jnp.inf, F32)
+            row_max = jnp.max(peak[i], axis=1, keepdims=True)
+            peak[i] = jnp.broadcast_to(row_max, (slots, lane_step))
+            total[...] = jnp.zeros((slots, lane_step), F32)
+            mixed[...] = jnp.zeros((slots, HEAD_DIM), F32)
 
             @pl.loop(0, 3)
             def _(part):
-                query = jnp.concatenate([work[k, i + 1, :, 0:HEAD_DIM], q_mask[i]], axis=1)
-                key = jnp.concatenate(
-                    [work[k, i + part, :, HEAD_DIM : 2 * HEAD_DIM], k_mask[i + part]], axis=1
-                )
-                found = matmul_t(query, key)
-                scores[part] = found
-                peak[...] = functools.reduce(
-                    jnp.maximum,
-                    [found[:, t * lane_step : (t + 1) * lane_step] for t in range(tiles)],
-                    peak[...],
-                )
-
-            row_max = jnp.max(peak[...], axis=1, keepdims=True)
-            peak[...] = jnp.broadcast_to(row_max, (slots, lane_step))
-            total[...] = jnp.zeros((slots, lane_step), F32)
-            mixed[...] = jnp.zeros((slots, HEAD_DIM), F32)
-
-            @pl.loop(0, 3)
-            def _(part):
-                row_max = peak[...]
+                row_max = peak[i]
                 weights = [
                     jnp.exp2(
-                        (scores[part, :, t * lane_step : (t + 1) * lane_step] - row_max)
+                        (scores[i, part, :, t * lane_step : (t + 1) * lane_step] - row_max)
                         * SCALE_LOG2
                     )
                     for t in range(tiles)
@@ -550,8 +555,8 @@
             vmem(tokens, slots),
             vmem(CORES, half, slots),
             vmem(slots, slots),
-            vmem(3, slots, slots, dtype=F32),
-            vmem(slots, lane_step, dtype=F32),
+            vmem(CORES, 3, slots, slots, dtype=F32),
+            vmem(CORES, slots, lane_step, dtype=F32),
             vmem(slots, lane_step, dtype=F32),
             vmem(slots, thin, dtype=F32),
             vmem(n_tok, thin),

time: 125 us -> 123 us (0.984)
  Pallas kernels: 123 us -> 121 us
    pallas_call x1, Pallas kernels: 123 us -> 121 us  [per_device(): pl.pallas_call(functools.partial(kernel, (nx, n_axis, per_pair, heads)),...]
where the time goes in v5:
time: 123 us
  Pallas kernels  121 us (98%)
  local copies, waits for them, and re-layouts  1.77 us (1%)
    pallas_call x1, Pallas kernels, per_device(): pl.pallas_call(functools.partial(kernel, (nx, n_axis, per_pair, heads)),...  121 us

profile of v5, /device:TPU:1, one launch (start us, length us, event | category | flops | bytes accessed | tf_op | source)
XLA Modules:
  0.0 123.1 jit_solution(9138455796335314108)
XLA Ops:
  0.0 121.3 %shard_map.64 = bf16[64,3072]{1,0:T(8,128)(2,1)} custom-call(bf16[64,3072]{1,0:T(8,128)(2,1)} %q_ref.1, bf16[64,3072]{1,0:T(8,128)(2,1)} %k_ref.1, bf16[64,3072]{1,0:T(8,128)(2,1)} %v_ref.1, s32[1,256]{1,0:T(1,128)} %bitcast.3, s32[1,512]{1,0:T(1,128)} %bitcast.2, s32[4,8]{1,0:T(4,128)} %pair_list.1), custom_call_target="tpu_custom_call" | custom-call | tf_op jit(solution)/shard_map/pallas_call | solution.py:537
  121.3 1.8 %copy.8 = bf16[64,3072]{1,0:T(8,128)(2,1)} copy(bf16[64,3072]{1,0:T(8,128)(2,1)} %shard_map.64) | data formatting | bytes 786432

commit v6 on v5

--- a/solution.py
+++ b/solution.py
@@ -14,7 +14,6 @@
 TILE = 16
 LANES = 8
 AHEAD = 2
-STEP = 1
 MASKED = -(2.0**100)
 SCALE_LOG2 = math.log2(math.e) / math.sqrt(HEAD_DIM)
 MESH = pl.DeviceIdType.MESH
@@ -23,7 +22,8 @@
 
 X_OWN, X_SEND, X_RECV, A_SEND, A_RECV, B_SEND, B_NEAR, B_RECV, H_SEND, H_RECV = range(10)
 RB_SEND, RB_RECV, RA_SEND, RA_RECV, RX_SEND, RX_OWN = range(10, 16)
-STAGES = 16
+A_VIA, A_ON, B_VIA, B_ON = range(16, 20)
+STAGES = 20
 
 
 def matmul(left, right):
@@ -48,7 +48,7 @@
 
 def kernel(
     dims, q_ref, k_ref, v_ref, cluster, owners, pair_list, out_ref,
-    x_recv, a_send, a_recv, b_send, work, o_send, o_recv, t_send, t_recv, x_back,
+    x_recv, a_send, a_recv, a_via, b_send, b_via, work, o_send, o_recv, t_send, t_recv, x_back,
     pick, pick_t, perm, perm_t, scores, peak, total, mixed,
     l_a_send, l_a_recv, l_b_send, l_b_recv, labels, mask_tile, mask_in, q_mask, k_mask,
     sem, label_sem, mask_sem, out_sem,
@@ -204,21 +204,53 @@
     lane = iota((n_tok, HEAD_DIM), 1)
     l_a_send[...] = jnp.where(lane % LANES == cl_dev, 1.0 - filled, filled).astype(BF16)
 
-    def first_hop(src, dst, send, recv, par, size):
+    half, half_way = n_axis // 2, n_axis // 4 * (1 - 2 * core)
+
+    def round_ring(here, step):
+        return lax.rem(here + n_axis + step, n_axis)
+
+    def first_hop(src, dst, send, recv, par, size, via=None, via_recv=None):
         a, b = place(par)
         pltpu.make_async_copy(src.at[block(a, size)], dst.at[block(a, size)], recv).start()
 
-        @pl.loop(1, n_axis)
-        def _(d):
-            other = lax.rem(a + d, n_axis)
+        def put(other):
             copy_to(
                 src.at[block(other, size)], dst.at[block(a, size)], send, recv,
                 device(other, b, core, par),
             )
 
-    def second_hop(src_at, dst, send, near, recv, par):
+        if via is None:
+            put(round_ring(a, half))
+        else:
+            copy_to(
+                src.at[block(round_ring(a, half), size)], via, send, via_recv,
+                device(round_ring(a, half_way), b, core, par),
+            )
+
+        @pl.loop(1, half)
+        def _(d):
+            put(round_ring(a, d))
+            put(round_ring(a, -d))
+
+    def second_hop(src_at, dst, send, near, recv, par, via=None, via_recv=None):
         a, b = place(par)
 
+        def put(other):
+            copy_to(src_at(other), dst, send, recv, device(a, other, par, par))
+
+        if via is None:
+            put(round_ring(b, half))
+        else:
+            copy_to(
+                src_at(round_ring(b, half)), via, send, via_recv,
+                device(a, round_ring(b, half_way), core, par),
+            )
+
+        @pl.loop(1, half)
+        def _(d):
+            put(round_ring(b, d))
+            put(round_ring(b, -d))
+
         @pl.when(core == par)
         def _():
             pltpu.make_async_copy(src_at(b), dst, recv).start()
@@ -227,10 +259,28 @@
         def _():
             copy_to(src_at(b), dst, near, recv, device(a, b, par, par))
 
-        @pl.loop(1, n_axis)
-        def _(d):
-            other = lax.rem(b + d, n_axis)
-            copy_to(src_at(other), dst, send, recv, device(a, other, par, par))
+    relayed = n_axis >= 4
+
+    def pass_first(h):
+        par = h % 2
+        a, b = place(par)
+        wait_bytes(a_via.at[h], sem.at[A_VIA, h])
+        copy_to(
+            a_via.at[h], a_recv.at[h, block(round_ring(a, -half_way), a_rows)],
+            sem.at[A_ON, h], sem.at[A_RECV, h],
+            device(round_ring(a, half_way), b, core, par),
+        )
+
+    def pass_second(h):
+        par = h % 2
+        a, b = place(par)
+        wait_bytes(b_via.at[h], sem.at[B_VIA, h])
+        origin = round_ring(b, -half_way) * CORES + core
+        copy_to(
+            b_via.at[h], work.at[h // 2, pl.ds(1, CORES), block(origin, b_rows)],
+            sem.at[B_ON, h], sem.at[B_RECV, h // 2],
+            device(a, round_ring(b, half_way), par, par),
+        )
 
     def source(par):
         _, b = place(par)
@@ -259,7 +309,10 @@
             part = block(i, slots // 2)
             a_send[h, part] = matmul(pick[part], x_recv[h]).astype(BF16)
 
-        first_hop(a_send.at[h], a_recv.at[h], sem.at[A_SEND, h], sem.at[A_RECV, h], h % 2, a_rows)
+        via = (a_via.at[h], sem.at[A_VIA, h]) if relayed else ()
+        first_hop(
+            a_send.at[h], a_recv.at[h], sem.at[A_SEND, h], sem.at[A_RECV, h], h % 2, a_rows, *via
+        )
 
     def turn(h):
         par = h % 2
@@ -269,10 +322,11 @@
         def _(i):
             b_send[h, i] = matmul(perm[i], a_recv[h]).astype(BF16)
 
+        via = (b_via.at[h], sem.at[B_VIA, h]) if relayed else ()
         second_hop(
             lambda other: b_send.at[h, :, block(other, b_rows)],
             work.at[h // 2, pl.ds(1, CORES), block(source(par), b_rows)],
-            sem.at[B_SEND, h], sem.at[B_NEAR, h], sem.at[B_RECV, h // 2], par,
+            sem.at[B_SEND, h], sem.at[B_NEAR, h], sem.at[B_RECV, h // 2], par, *via,
         )
 
     def share(k):
@@ -457,12 +511,15 @@
 
         return pair
 
-    stages = (both(pack), both(turn), share, attend, both(turn_back), both(finish))
-
-    @pl.loop(0, mine + STEP * (len(stages) - 1))
+    stages = [(0, both(pack)), (1, both(turn)), (2, share), (4, both(turn_back))]
+    stages += [(5, both(finish)), (3, attend)]
+    if relayed:
+        stages.insert(3, (1, both(pass_second)))
+        stages.insert(2, (0, both(pass_first)))
+
+    @pl.loop(0, mine + 5)
     def _(step):
-        for number, stage in enumerate(stages):
-            lag = STEP * number
+        for number, (lag, stage) in enumerate(stages):
 
             @pl.when((step >= lag) & (step < mine + lag))
             def _():
@@ -493,6 +550,10 @@
         wait_bytes(t_send.at[h, others_a], sem.at[RA_SEND, h])
         wait_bytes(x_back.at[h, pl.ds(0, tokens - rows)], sem.at[RX_SEND, h])
         wait_bytes(x_back.at[h, pl.ds(0, rows)], sem.at[RX_OWN, h])
+
+        if relayed:
+            wait_bytes(a_via.at[h], sem.at[A_ON, h])
+            wait_bytes(b_via.at[h], sem.at[B_ON, h])
 
         @pl.when(core != h % 2)
         def _():
@@ -544,7 +605,9 @@
             vmem(heads, tokens, wide),
             vmem(heads, slots, wide),
             vmem(heads, slots, wide),
+            vmem(heads, line * per_pair, wide),
             vmem(heads, CORES, half, wide),
+            vmem(heads, CORES, n_axis * per_pair, wide),
             vmem(mine, sides, slots, wide),
             vmem(mine, CORES, slots, thin),
             vmem(heads, CORES, half, thin),

time: 123 us -> 133 us (1.081)
  Pallas kernels: 121 us -> 130 us
    pallas_call x1, Pallas kernels: 121 us -> 130 us  [per_device(): pl.pallas_call(functools.partial(kernel, (nx, n_axis, per_pair, heads)),...]
where the time goes in v6:
time: 133 us; the launch traced here: 132 us
  Pallas kernels  130 us (98%)
  local copies, waits for them, and re-layouts  1.77 us (1%)
    pallas_call x1, Pallas kernels, per_device(): pl.pallas_call(functools.partial(kernel, (nx, n_axis, per_pair, heads)),...  130 us

profile of v6, /device:TPU:1, one launch (start us, length us, event | category | flops | bytes accessed | tf_op | source)
XLA Modules:
  0.0 131.8 jit_solution(2849244301925058802)
XLA Ops:
  0.0 130.0 %shard_map.64 = bf16[64,3072]{1,0:T(8,128)(2,1)} custom-call(bf16[64,3072]{1,0:T(8,128)(2,1)} %q_ref.1, bf16[64,3072]{1,0:T(8,128)(2,1)} %k_ref.1, bf16[64,3072]{1,0:T(8,128)(2,1)} %v_ref.1, s32[1,256]{1,0:T(1,128)} %bitcast.3, s32[1,512]{1,0:T(1,128)} %bitcast.2, s32[4,8]{1,0:T(4,128)} %pair_list.1), custom_call_target="tpu_custom_call" | custom-call | tf_op jit(solution)/shard_map/pallas_call | solution.py:598
  130.1 1.8 %copy.8 = bf16[64,3072]{1,0:T(8,128)(2,1)} copy(bf16[64,3072]{1,0:T(8,128)(2,1)} %shard_map.64) | data formatting | bytes 786432

commit v7 on v5

--- a/solution.py
+++ b/solution.py
@@ -14,7 +14,6 @@
 TILE = 16
 LANES = 8
 AHEAD = 2
-STEP = 1
 MASKED = -(2.0**100)
 SCALE_LOG2 = math.log2(math.e) / math.sqrt(HEAD_DIM)
 MESH = pl.DeviceIdType.MESH
@@ -147,39 +146,12 @@
                     (tok, other),
                 )
 
+        for kind, ref in enumerate((q_ref, k_ref, v_ref)):
+            own_copy(ref, kind, h).start()
+
     @pl.loop(0, min(AHEAD, heads))
     def _(h):
         spread(h)
-
-    @pl.loop(0, heads)
-    def _(h):
-        for kind, ref in enumerate((q_ref, k_ref, v_ref)):
-            own_copy(ref, kind, h).start()
-
-    pair_local = pair_list[...] - (tok - core - 1) * cl_dev
-    lane = iota((cl_dev, HEAD_DIM), 1)
-    allowed = lane > invalid
-    for j in range(pairs):
-        allowed = allowed | (pair_local[:, j : j + 1] == lane)
-    mask_tile[...] = jnp.concatenate(
-        [jnp.where(allowed, 0.0, MASKED), jnp.zeros((TILE - cl_dev, HEAD_DIM), F32)], axis=0
-    ).astype(BF16)
-
-    keepers = [(z * n_axis + y) * CORES, (y * n_axis + z) * CORES + 1]
-    for end, keeper in enumerate(keepers):
-
-        @pl.when(tok == keeper)
-        def _():
-            pltpu.make_async_copy(
-                mask_tile, mask_in.at[core], mask_sem.at[CORES + core]
-            ).start()
-
-        @pl.when(tok != keeper)
-        def _():
-            copy_to(
-                mask_tile, mask_in.at[core], mask_sem.at[end], mask_sem.at[CORES + core],
-                (keeper, my_x),
-            )
 
     clusters = owners.shape[1]
     cluster_hot = one_hot(iota((clusters, tokens), 0) == cluster[...])
@@ -199,11 +171,6 @@
     def _(i):
         pick[block(i, chunk)] = one_hot(iota((chunk, tokens), 0) + i * chunk == send_row)
 
-    lane = iota((HEAD_DIM, tokens), 0) - rank * LANES
-    filled = matmul_t(target_hot, one_hot((lane == local_id) | (lane == cl_dev)))
-    lane = iota((n_tok, HEAD_DIM), 1)
-    l_a_send[...] = jnp.where(lane % LANES == cl_dev, 1.0 - filled, filled).astype(BF16)
-
     def first_hop(src, dst, send, recv, par, size):
         a, b = place(par)
         pltpu.make_async_copy(src.at[block(a, size)], dst.at[block(a, size)], recv).start()
@@ -239,11 +206,6 @@
     others_a = pl.ds(0, slots - a_rows)
     others_b = pl.ds(0, b_rows * (n_axis - 1))
     label_others = pl.ds(0, n_tok - line)
-
-    for par in range(CORES):
-        first_hop(
-            l_a_send, l_a_recv.at[par], label_sem.at[0, par], label_sem.at[1, par], par, line
-        )
 
     def pack(h):
         for kind, ref in enumerate((q_ref, k_ref, v_ref)):
@@ -377,6 +339,43 @@
                 sem.at[RX_SEND, h], out_sem, (tok, other),
             )
 
+    keepers = [(z * n_axis + y) * CORES, (y * n_axis + z) * CORES + 1]
+
+    def send_labels():
+        pair_local = pair_list[...] - (tok - core - 1) * cl_dev
+        lane = iota((cl_dev, HEAD_DIM), 1)
+        allowed = lane > invalid
+        for j in range(pairs):
+            allowed = allowed | (pair_local[:, j : j + 1] == lane)
+        mask_tile[...] = jnp.concatenate(
+            [jnp.where(allowed, 0.0, MASKED), jnp.zeros((TILE - cl_dev, HEAD_DIM), F32)], axis=0
+        ).astype(BF16)
+
+        for end, keeper in enumerate(keepers):
+
+            @pl.when(tok == keeper)
+            def _():
+                pltpu.make_async_copy(
+                    mask_tile, mask_in.at[core], mask_sem.at[CORES + core]
+                ).start()
+
+            @pl.when(tok != keeper)
+            def _():
+                copy_to(
+                    mask_tile, mask_in.at[core], mask_sem.at[end], mask_sem.at[CORES + core],
+                    (keeper, my_x),
+                )
+
+        lane = iota((HEAD_DIM, tokens), 0) - rank * LANES
+        filled = matmul_t(target_hot, one_hot((lane == local_id) | (lane == cl_dev)))
+        lane = iota((n_tok, HEAD_DIM), 1)
+        l_a_send[...] = jnp.where(lane % LANES == cl_dev, 1.0 - filled, filled).astype(BF16)
+
+        for par in range(CORES):
+            first_hop(
+                l_a_send, l_a_recv.at[par], label_sem.at[0, par], label_sem.at[1, par], par, line
+            )
+
     def make_perms():
         half = slots // CORES
 
@@ -457,12 +456,12 @@
 
         return pair
 
-    stages = (both(pack), both(turn), share, attend, both(turn_back), both(finish))
-
-    @pl.loop(0, mine + STEP * (len(stages) - 1))
+    stages = [(0, both(pack)), (1, both(turn)), (2, share), (4, both(turn_back))]
+    stages += [(5, both(finish)), (3, attend)]
+
+    @pl.loop(0, mine + 5)
     def _(step):
-        for number, stage in enumerate(stages):
-            lag = STEP * number
+        for number, (lag, stage) in enumerate(stages):
 
             @pl.when((step >= lag) & (step < mine + lag))
             def _():
@@ -472,6 +471,7 @@
 
                 @pl.when(step == 0)
                 def _():
+                    send_labels()
                     make_perms()
                     turn_labels()
 

time: 123 us -> 137 us (1.11)
  Pallas kernels: 121 us -> 135 us
    pallas_call x1, Pallas kernels: 121 us -> 135 us  [per_device(): pl.pallas_call(functools.partial(kernel, (nx, n_axis, per_pair, heads)),...]
where the time goes in v7:
time: 137 us
  Pallas kernels  135 us (99%)
  local copies, waits for them, and re-layouts  1.77 us (1%)
    pallas_call x1, Pallas kernels, per_device(): pl.pallas_call(functools.partial(kernel, (nx, n_axis, per_pair, heads)),...  135 us

profile of v7, /device:TPU:1, one launch (start us, length us, event | category | flops | bytes accessed | tf_op | source)
XLA Modules:
  0.0 136.5 jit_solution(14379508302637433101)
XLA Ops:
  0.0 134.7 %shard_map.64 = bf16[64,3072]{1,0:T(8,128)(2,1)} custom-call(bf16[64,3072]{1,0:T(8,128)(2,1)} %q_ref.1, bf16[64,3072]{1,0:T(8,128)(2,1)} %k_ref.1, bf16[64,3072]{1,0:T(8,128)(2,1)} %v_ref.1, s32[1,256]{1,0:T(1,128)} %bitcast.3, s32[1,512]{1,0:T(1,128)} %bitcast.2, s32[4,8]{1,0:T(4,128)} %pair_list.1), custom_call_target="tpu_custom_call" | custom-call | tf_op jit(solution)/shard_map/pallas_call | solution.py:537
  134.7 1.8 %copy.8 = bf16[64,3072]{1,0:T(8,128)(2,1)} copy(bf16[64,3072]{1,0:T(8,128)(2,1)} %shard_map.64) | data formatting | bytes 786432

commit v8 on v7

--- a/solution.py
+++ b/solution.py
@@ -14,6 +14,7 @@
 TILE = 16
 LANES = 8
 AHEAD = 2
+STEP = 1
 MASKED = -(2.0**100)
 SCALE_LOG2 = math.log2(math.e) / math.sqrt(HEAD_DIM)
 MESH = pl.DeviceIdType.MESH
@@ -171,33 +172,59 @@
     def _(i):
         pick[block(i, chunk)] = one_hot(iota((chunk, tokens), 0) + i * chunk == send_row)
 
-    def first_hop(src, dst, send, recv, par, size):
-        a, b = place(par)
-        pltpu.make_async_copy(src.at[block(a, size)], dst.at[block(a, size)], recv).start()
-
-        @pl.loop(1, n_axis)
+    lane = iota((HEAD_DIM, tokens), 0) - rank * LANES
+    filled = matmul_t(target_hot, one_hot((lane == local_id) | (lane == cl_dev)))
+    lane = iota((n_tok, HEAD_DIM), 1)
+    l_a_send[...] = jnp.where(lane % LANES == cl_dev, 1.0 - filled, filled).astype(BF16)
+
+    half_ring = n_axis // 2
+
+    def round_ring(here, step):
+        return lax.rem(here + n_axis + step, n_axis)
+
+    def interleave(puts):
+        @pl.loop(1, half_ring)
         def _(d):
-            other = lax.rem(a + d, n_axis)
-            copy_to(
-                src.at[block(other, size)], dst.at[block(a, size)], send, recv,
-                device(other, b, core, par),
-            )
-
-    def second_hop(src_at, dst, send, near, recv, par):
-        a, b = place(par)
-
-        @pl.when(core == par)
-        def _():
-            pltpu.make_async_copy(src_at(b), dst, recv).start()
-
-        @pl.when(core != par)
-        def _():
-            copy_to(src_at(b), dst, near, recv, device(a, b, par, par))
-
-        @pl.loop(1, n_axis)
-        def _(d):
-            other = lax.rem(b + d, n_axis)
-            copy_to(src_at(other), dst, send, recv, device(a, other, par, par))
+            for step in (d, -d):
+                for put, here in puts:
+                    put(round_ring(here, step))
+
+        for put, here in puts:
+            put(round_ring(here, half_ring))
+
+    def first_hops(hops, size):
+        def start(par, src, dst, send, recv):
+            a, b = place(par)
+            pltpu.make_async_copy(src.at[block(a, size)], dst.at[block(a, size)], recv).start()
+
+            def put(other):
+                copy_to(
+                    src.at[block(other, size)], dst.at[block(a, size)], send, recv,
+                    device(other, b, core, par),
+                )
+
+            return put, a
+
+        interleave([start(par, *hop) for par, hop in enumerate(hops)])
+
+    def second_hops(hops):
+        def start(par, src_at, dst, send, near, recv):
+            a, b = place(par)
+
+            @pl.when(core == par)
+            def _():
+                pltpu.make_async_copy(src_at(b), dst, recv).start()
+
+            @pl.when(core != par)
+            def _():
+                copy_to(src_at(b), dst, near, recv, device(a, b, par, par))
+
+            def put(other):
+                copy_to(src_at(other), dst, send, recv, device(a, other, par, par))
+
+            return put, b
+
+        interleave([start(par, *hop) for par, hop in enumerate(hops)])
 
     def source(par):
         _, b = place(par)
@@ -206,6 +233,15 @@
     others_a = pl.ds(0, slots - a_rows)
     others_b = pl.ds(0, b_rows * (n_axis - 1))
     label_others = pl.ds(0, n_tok - line)
+
+    both = range(CORES)
+    first_hops(
+        [
+            (l_a_send, l_a_recv.at[par], label_sem.at[0, par], label_sem.at[1, par])
+            for par in both
+        ],
+        line,
+    )
 
     def pack(h):
         for kind, ref in enumerate((q_ref, k_ref, v_ref)):
@@ -221,21 +257,38 @@
             part = block(i, slots // 2)
             a_send[h, part] = matmul(pick[part], x_recv[h]).astype(BF16)
 
-        first_hop(a_send.at[h], a_recv.at[h], sem.at[A_SEND, h], sem.at[A_RECV, h], h % 2, a_rows)
-
     def turn(h):
-        par = h % 2
         wait_bytes(a_recv.at[h], sem.at[A_RECV, h])
 
         @pl.loop(0, CORES)
         def _(i):
             b_send[h, i] = matmul(perm[i], a_recv[h]).astype(BF16)
 
-        second_hop(
-            lambda other: b_send.at[h, :, block(other, b_rows)],
-            work.at[h // 2, pl.ds(1, CORES), block(source(par), b_rows)],
-            sem.at[B_SEND, h], sem.at[B_NEAR, h], sem.at[B_RECV, h // 2], par,
-        )
+    def way_of(src, dst, send, recv):
+        def stage(k):
+            first_hops(
+                [
+                    (src.at[h], dst.at[h], sem.at[send, h], sem.at[recv, h])
+                    for h in (CORES * k + par for par in both)
+                ],
+                a_rows,
+            )
+
+        return stage
+
+    send_a = way_of(a_send, a_recv, A_SEND, A_RECV)
+    send_ra = way_of(t_send, t_recv, RA_SEND, RA_RECV)
+
+    def send_b(k):
+        def hop(par):
+            h = CORES * k + par
+            return (
+                lambda other: b_send.at[h, :, block(other, b_rows)],
+                work.at[k, pl.ds(1, CORES), block(source(par), b_rows)],
+                sem.at[B_SEND, h], sem.at[B_NEAR, h], sem.at[B_RECV, k],
+            )
+
+        second_hops([hop(par) for par in both])
 
     def share(k):
         wait_bytes(work.at[k, pl.ds(1, CORES)], sem.at[B_RECV, k])
@@ -319,9 +372,6 @@
     def turn_back(h):
         wait_bytes(o_recv.at[h], sem.at[RB_RECV, h])
         t_send[h] = matmul(perm_t[...], o_recv[h].reshape(slots, HEAD_DIM)).astype(BF16)
-        first_hop(
-            t_send.at[h], t_recv.at[h], sem.at[RA_SEND, h], sem.at[RA_RECV, h], h % 2, a_rows
-        )
 
     def finish(h):
         wait_bytes(t_recv.at[h], sem.at[RA_RECV, h])
@@ -341,7 +391,7 @@
 
     keepers = [(z * n_axis + y) * CORES, (y * n_axis + z) * CORES + 1]
 
-    def send_labels():
+    def send_masks():
         pair_local = pair_list[...] - (tok - core - 1) * cl_dev
         lane = iota((cl_dev, HEAD_DIM), 1)
         allowed = lane > invalid
@@ -366,16 +416,6 @@
                     (keeper, my_x),
                 )
 
-        lane = iota((HEAD_DIM, tokens), 0) - rank * LANES
-        filled = matmul_t(target_hot, one_hot((lane == local_id) | (lane == cl_dev)))
-        lane = iota((n_tok, HEAD_DIM), 1)
-        l_a_send[...] = jnp.where(lane % LANES == cl_dev, 1.0 - filled, filled).astype(BF16)
-
-        for par in range(CORES):
-            first_hop(
-                l_a_send, l_a_recv.at[par], label_sem.at[0, par], label_sem.at[1, par], par, line
-            )
-
     def make_perms():
         half = slots // CORES
 
@@ -400,14 +440,18 @@
         row, column = iota((n_tok, n_tok), 0), iota((n_tok, n_tok), 1)
         start = (row // CORES) % n_axis * line + row // line * CORES + row % CORES
         turned = one_hot(start == column)
-        for par in range(CORES):
+        for par in both:
             wait_bytes(l_a_recv.at[par], label_sem.at[1, par])
             l_b_send[par] = matmul(turned, l_a_recv[par]).astype(BF16)
-            second_hop(
+
+        def hop(par):
+            return (
                 lambda other: l_b_send.at[par, block(other, line)],
                 l_b_recv.at[block(source(par), line)],
-                label_sem.at[2, par], label_sem.at[3, par], label_sem.at[4, 0], par,
-            )
+                label_sem.at[2, par], label_sem.at[3, par], label_sem.at[4, 0],
+            )
+
+        second_hops([hop(par) for par in both])
 
     def share_labels():
         wait_bytes(l_b_recv, label_sem.at[4, 0])
@@ -448,20 +492,26 @@
                 mask = jnp.concatenate([mask_in[side - 1], rest], axis=0)
                 q_mask[side - 1] = matmul(label, mask).astype(BF16)
 
-    def both(stage):
-        def pair(k):
+    def pair(stage, send=None):
+        def stage_of_pair(k):
             @pl.loop(CORES * k, CORES * k + CORES)
             def _(h):
                 stage(h)
 
-        return pair
-
-    stages = [(0, both(pack)), (1, both(turn)), (2, share), (4, both(turn_back))]
-    stages += [(5, both(finish)), (3, attend)]
-
-    @pl.loop(0, mine + 5)
+            if send is not None:
+                send(k)
+
+        return stage_of_pair
+
+    stages = (
+        pair(pack, send_a), pair(turn, send_b), share, attend,
+        pair(turn_back, send_ra), pair(finish),
+    )
+
+    @pl.loop(0, mine + STEP * (len(stages) - 1))
     def _(step):
-        for number, (lag, stage) in enumerate(stages):
+        for number, stage in enumerate(stages):
+            lag = STEP * number
 
             @pl.when((step >= lag) & (step < mine + lag))
             def _():
@@ -471,9 +521,9 @@
 
                 @pl.when(step == 0)
                 def _():
-                    send_labels()
                     make_perms()
                     turn_labels()
+                    send_masks()
 
         @pl.when(step == 1)
         def _():

time: 137 us -> 126 us (0.920)
  Pallas kernels: 135 us -> 123 us
    pallas_call x1, Pallas kernels: 135 us -> 123 us  [per_device(): pl.pallas_call(functools.partial(kernel, (nx, n_axis, per_pair, heads)),...]
where the time goes in v8:
time: 126 us; the launch traced here: 125 us
  Pallas kernels  123 us (98%)
  local copies, waits for them, and re-layouts  1.77 us (1%)
    pallas_call x1, Pallas kernels, per_device(): pl.pallas_call(functools.partial(kernel, (nx, n_axis, per_pair, heads)),...  123 us

profile of v8, /device:TPU:1, one launch (start us, length us, event | category | flops | bytes accessed | tf_op | source)
XLA Modules:
  0.0 125.2 jit_solution(2207409039342896839)
XLA Ops:
  0.0 123.4 %shard_map.64 = bf16[64,3072]{1,0:T(8,128)(2,1)} custom-call(bf16[64,3072]{1,0:T(8,128)(2,1)} %q_ref.1, bf16[64,3072]{1,0:T(8,128)(2,1)} %k_ref.1, bf16[64,3072]{1,0:T(8,128)(2,1)} %v_ref.1, s32[1,256]{1,0:T(1,128)} %bitcast.3, s32[1,512]{1,0:T(1,128)} %bitcast.2, s32[4,8]{1,0:T(4,128)} %pair_list.1), custom_call_target="tpu_custom_call" | custom-call | tf_op jit(solution)/shard_map/pallas_call | solution.py:587
  123.4 1.8 %copy.8 = bf16[64,3072]{1,0:T(8,128)(2,1)} copy(bf16[64,3072]{1,0:T(8,128)(2,1)} %shard_map.64) | data formatting | bytes 786432

commit v9 on v5

--- a/solution.py
+++ b/solution.py
@@ -356,7 +356,13 @@
 
     def turn_back(h):
         wait_bytes(o_recv.at[h], sem.at[RB_RECV, h])
-        t_send[h] = matmul(perm_t[...], o_recv[h].reshape(slots, HEAD_DIM)).astype(BF16)
+
+        @pl.loop(0, 2)
+        def _(i):
+            part = block(i, slots // 2)
+            returned = o_recv[h].reshape(slots, HEAD_DIM)
+            t_send[h, part] = matmul(perm_t[part], returned).astype(BF16)
+
         first_hop(
             t_send.at[h], t_recv.at[h], sem.at[RA_SEND, h], sem.at[RA_RECV, h], h % 2, a_rows
         )
@@ -384,13 +390,15 @@
             r, a, b = row % per_pair, (row // per_pair) % n_axis, row // b_rows
             return a * a_rows + b * (CORES * per_pair) + i * per_pair + r
 
-        for i in range(CORES):
-            perm[i] = one_hot(source_of(iota((half, slots), 0), i) == iota((half, slots), 1))
-
-        @pl.loop(0, slots // chunk)
+        piece = min(chunk, half)
+
+        @pl.loop(0, slots // piece)
         def _(part):
-            row, column = iota((chunk, slots), 0) + part * chunk, iota((chunk, slots), 1)
-            perm_t[block(part, chunk)] = one_hot(
+            row, column = iota((piece, slots), 0) + part * piece, iota((piece, slots), 1)
+            i, start = part * piece // half, part * piece % half
+            rows_here = pl.ds(pl.multiple_of(start, piece), piece)
+            perm[i, rows_here] = one_hot(source_of(row % half, i) == column)
+            perm_t[block(part, piece)] = one_hot(
                 source_of(column % half, column // half) == row
             )
 
@@ -429,25 +437,29 @@
             wait_bytes(mask_in.at[c], mask_sem.at[CORES + c])
         row, column = iota((HEAD_DIM, HEAD_DIM), 0), iota((HEAD_DIM, HEAD_DIM), 1)
         fold = one_hot((row % LANES == column) & (row < per_pair * LANES))
-        owner_row = one_hot(iota((slots, n_tok), 0) // per_pair == iota((slots, n_tok), 1))
-        shape = (slots, HEAD_DIM)
-        own_lanes = iota(shape, 1) // LANES == iota(shape, 0) % per_pair
         rest = jnp.zeros((HEAD_DIM - TILE, HEAD_DIM), BF16)
-
-        @pl.loop(0, sides)
-        def _(side):
+        piece = min(chunk, slots)
+
+        @pl.loop(0, sides * (slots // piece))
+        def _(n):
+            side, start = n // (slots // piece), n % (slots // piece) * piece
+            here = pl.ds(pl.multiple_of(start, piece), piece)
+            owner = (iota((piece, n_tok), 0) + start) // per_pair
+            owner_row = one_hot(owner == iota((piece, n_tok), 1))
+            shape = (piece, HEAD_DIM)
+            own_lanes = iota(shape, 1) // LANES == iota(shape, 0) % per_pair
             spaced = jnp.where(own_lanes, matmul(owner_row, labels[side]), 0.0).astype(BF16)
             label = matmul(spaced, fold).astype(BF16)
             shift = one_hot(
                 ((row < cl_dev) & (column == row + cl_dev * side))
                 | ((row == cl_dev) & (column == invalid))
             )
-            k_mask[side] = matmul(label, shift).astype(BF16)
+            k_mask[side, here] = matmul(label, shift).astype(BF16)
 
             @pl.when((side >= 1) & (side <= CORES))
             def _():
                 mask = jnp.concatenate([mask_in[side - 1], rest], axis=0)
-                q_mask[side - 1] = matmul(label, mask).astype(BF16)
+                q_mask[side - 1, here] = matmul(label, mask).astype(BF16)
 
     def both(stage):
         def pair(k):
@@ -574,7 +586,7 @@
             pltpu.SemaphoreType.DMA,
         ],
         compiler_params=pltpu.CompilerParams(
-            collective_id=0, has_side_effects=True, vmem_limit_bytes=60 * 2**20
+            collective_id=0, has_side_effects=True, vmem_limit_bytes=int(53.3 * 2**20)
         ),
     )(queries, key_rows, values, cluster[None, :], owners[None, :], pair_list)
 

time: 123 us -> 124 us (level)
  no operation moved by 1% of the time
where the time goes in v9:
time: 124 us
  Pallas kernels  121 us (98%)
  local copies, waits for them, and re-layouts  2.12 us (2%)
    pallas_call x1, Pallas kernels, per_device(): pl.pallas_call(functools.partial(kernel, (nx, n_axis, per_pair, heads)),...  121 us

profile of v9, /device:TPU:1, one launch (start us, length us, event | category | flops | bytes accessed | tf_op | source)
XLA Modules:
  0.0 123.6 jit_solution(17224353759227571098)
XLA Ops:
  0.0 0.0 copy-start
  0.0 0.0 copy-start.2
  0.0 0.7 copy-done
  0.7 0.0 copy-done.2
  0.7 0.0 copy-start.1
  0.7 0.7 copy-done.1
  1.4 121.4 %shard_map.64 = bf16[64,3072]{1,0:T(8,128)(2,1)S(1)} custom-call(bf16[64,3072]{1,0:T(8,128)(2,1)} %q_ref.1, bf16[64,3072]{1,0:T(8,128)(2,1)} %k_ref.1, bf16[64,3072]{1,0:T(8,128)(2,1)} %v_ref.1, s32[1,256]{1,0:T(1,128)S(1)} %bitcast.3, s32[1,512]{1,0:T(1,128)S(1)} %bitcast.2, s32[4,8]{1,0:T(4,128)S(1)} %copy-done.1), custom_call_target="tpu_custom_call" | custom-call | tf_op jit(solution)/shard_map/pallas_call | solution.py:549
  122.8 0.7 copy.8
Async XLA Ops:
  0.0 0.7 copy-start
  0.0 0.7 copy-start.2
  0.7 0.7 copy-start.1

commit v10 on v9

--- a/solution.py
+++ b/solution.py
@@ -586,7 +586,7 @@
             pltpu.SemaphoreType.DMA,
         ],
         compiler_params=pltpu.CompilerParams(
-            collective_id=0, has_side_effects=True, vmem_limit_bytes=int(53.3 * 2**20)
+            collective_id=0, has_side_effects=True, vmem_limit_bytes=60 * 2**20
         ),
     )(queries, key_rows, values, cluster[None, :], owners[None, :], pair_list)
 

time: 124 us -> 124 us (level)
  no operation moved by 1% of the time
where the time goes in v10:
time: 124 us
  Pallas kernels  122 us (98%)
  local copies, waits for them, and re-layouts  1.77 us (1%)
    pallas_call x1, Pallas kernels, per_device(): pl.pallas_call(functools.partial(kernel, (nx, n_axis, per_pair, heads)),...  122 us

profile of v10, /device:TPU:1, one launch (start us, length us, event | category | flops | bytes accessed | tf_op | source)
XLA Modules:
  0.0 123.9 jit_solution(9124358327180034365)
XLA Ops:
  0.0 122.2 %shard_map.64 = bf16[64,3072]{1,0:T(8,128)(2,1)} custom-call(bf16[64,3072]{1,0:T(8,128)(2,1)} %q_ref.1, bf16[64,3072]{1,0:T(8,128)(2,1)} %k_ref.1, bf16[64,3072]{1,0:T(8,128)(2,1)} %v_ref.1, s32[1,256]{1,0:T(1,128)} %bitcast.3, s32[1,512]{1,0:T(1,128)} %bitcast.2, s32[4,8]{1,0:T(4,128)} %pair_list.1), custom_call_target="tpu_custom_call" | custom-call | tf_op jit(solution)/shard_map/pallas_call | solution.py:549
  122.2 1.8 %copy.8 = bf16[64,3072]{1,0:T(8,128)(2,1)} copy(bf16[64,3072]{1,0:T(8,128)(2,1)} %shard_map.64) | data formatting | bytes 786432
